TPU v7x, 512 devices: a whole 4x8x8 slice. The times are simulated.
512 devices in a mesh: leaf: 32 (over z_hi, y), expert: 8 (over x, core), mp: 2 (over z_lo).
Axes of the slice: x: 4, y: 8, z: 8 (z_hi: 4, z_lo: 2; z = z_hi * 2 + z_lo), core: 2. Of those that a mesh axis runs over, the one named last changes fastest.
Arguments:
- node_cache: bfloat16 [32, 8, 2, 256, 128], P('leaf', 'expert'), may hold values from -30 to 30
- node_hidden: bfloat16 [32, 6144], P('leaf', ('expert', 'mp')), may hold values from -6 to 6
- node_slot: int32 [32], replicated, may hold values from 0 to 31, each once
- parent: int32 [64], replicated, may hold values from 0 to 31, as said below
- child_query: bfloat16 [64, 4, 48, 128], P('leaf', None, ('expert', 'mp')), may hold values from -40 to 40
- child_kv: bfloat16 [64, 8, 2, 4, 128], P('leaf', 'expert'), may hold values from -6 to 6
- routes: int32 [64, 4, 2], P('leaf'), may hold values from 0 to 7, all different within a row; in each aligned block of 8 rows (0 to 7, 8 to 15, ..., all dimensions but the last counted through in order) at most 4 rows name the same one
- gate_w: float32 [64, 4, 2], P('leaf'), may hold values from 0.2 to 1
- w_gate: bfloat16 [8, 6144, 8192], P('expert', None, ('leaf', 'mp')), may hold values from -0.078125 to 0.078125
- w_up: bfloat16 [8, 6144, 8192], P('expert', None, ('leaf', 'mp')), may hold values from -0.078125 to 0.078125
- w_down: bfloat16 [8, 8192, 6144], P('expert', ('leaf', 'mp')), may hold values from -0.0625 to 0.0625
Outputs:
- mixed: bfloat16 [64, 4, 6144], P('leaf', None, ('expert', 'mp'))
Inputs may be any that keep to these rules, and one draw needn't show every extreme that they name: `parent`: exactly 4 distinct node ids occur. `routes`: the two experts of a token differ; among the 8 tokens of one leaf index no expert is named more than 4 times.
All inputs are finite; a program needn't handle non-finite values.
Results may differ from a plain program's by a relative error of at most 0.013.
Values may be sent and summed in bfloat16 or wider, within the bound.
A program may use at most 64 MiB of HBM per device.

v0:
```python
import jax
import jax.numpy as jnp
from jax import lax
from jax.sharding import PartitionSpec as P

HQ = 48
KVH = 8
EXPERTS = 8
SLOT = 2


def local(
    node_cache,
    node_hidden,
    node_slot,
    parent,
    child_query,
    child_kv,
    routes,
    gate_w,
    w_gate,
    w_up,
    w_down,
):
    child_dev = child_query.shape[0]
    steps_here = child_query.shape[1]
    heads_loc = child_query.shape[2]
    head_size = child_query.shape[3]
    kv_loc = node_cache.shape[1]
    width_loc = node_hidden.shape[1]
    leaf_index = lax.axis_index("leaf")
    my_parents = lax.dynamic_slice_in_dim(parent, leaf_index * child_dev, child_dev)
    parent_rows = jnp.take(node_slot, my_parents)
    cache_piece = lax.all_gather(node_cache, "leaf", axis=0, tiled=True)
    hidden_piece = lax.all_gather(node_hidden, "leaf", axis=0, tiled=True)
    piece_rows = cache_piece.shape[0]
    select = (parent_rows[:, None] == jnp.arange(piece_rows)[None, :]).astype(jnp.bfloat16)
    got_cache = jnp.einsum(
        "cn,nkxpd->ckxpd", select, cache_piece, preferred_element_type=jnp.float32
    )
    got_hidden = jnp.dot(select, hidden_piece, preferred_element_type=jnp.float32)
    parent_cache = got_cache.astype(jnp.bfloat16)
    parent_row = got_hidden.astype(jnp.bfloat16)
    expert_index = lax.axis_index("expert")
    mp_size = lax.axis_size("mp")
    group = HQ // KVH
    head_ids = (expert_index * mp_size + lax.axis_index("mp")) * heads_loc + jnp.arange(
        heads_loc, dtype=jnp.int32
    )
    kv_of_head = head_ids // group - expert_index * kv_loc
    keys_old = jnp.take(parent_cache[:, :, 0], kv_of_head, axis=1)
    values_old = jnp.take(parent_cache[:, :, 1], kv_of_head, axis=1)
    keys_new = jnp.take(child_kv[:, :, 0], kv_of_head, axis=1)
    values_new = jnp.take(child_kv[:, :, 1], kv_of_head, axis=1)
    scale = 1.0 / head_size**0.5
    scores_old = (
        jnp.einsum("cshd,chpd->cshp", child_query, keys_old, preferred_element_type=jnp.float32)
        * scale
    )
    scores_new = (
        jnp.einsum("cshd,chud->cshu", child_query, keys_new, preferred_element_type=jnp.float32)
        * scale
    )
    allowed = jnp.arange(steps_here)[None, :] <= jnp.arange(steps_here)[:, None]
    scores_new = jnp.where(allowed[None, :, None, :], scores_new, -1e30)
    row_max = jnp.maximum(
        jnp.max(scores_old, axis=-1, keepdims=True), jnp.max(scores_new, axis=-1, keepdims=True)
    )
    expon_old = jnp.exp(scores_old - row_max)
    expon_new = jnp.exp(scores_new - row_max)
    denom = jnp.sum(expon_old, axis=-1, keepdims=True) + jnp.sum(expon_new, axis=-1, keepdims=True)
    probs_old = (expon_old / denom).astype(jnp.bfloat16)
    probs_new = (expon_new / denom).astype(jnp.bfloat16)
    attn = jnp.einsum("cshp,chpd->cshd", probs_old, values_old, preferred_element_type=jnp.float32)
    attn = attn + jnp.einsum(
        "cshu,chud->cshd", probs_new, values_new, preferred_element_type=jnp.float32
    )
    attn = attn.reshape(child_dev, steps_here, heads_loc * head_size)
    hidden_x = (parent_row.astype(jnp.float32)[:, None, :] + attn).astype(jnp.bfloat16)
    row_count = child_dev * steps_here
    x_rows = hidden_x.reshape(row_count, width_loc)
    route_flat = routes.reshape(row_count * 2)
    gate_values = gate_w.reshape(row_count * 2)
    order = jnp.arange(row_count * 2)
    earlier = (route_flat[:, None] == route_flat[None, :]) & (order[None, :] < order[:, None])
    slot_rank = jnp.sum(earlier.astype(jnp.int32), axis=1)
    expert_size = lax.axis_size("expert")
    exp_loc = EXPERTS // expert_size
    slot_half = slot_rank // SLOT
    target = (
        (route_flat // exp_loc * mp_size + slot_half) * (exp_loc * SLOT)
        + route_flat % exp_loc * SLOT
        + slot_rank % SLOT
    )
    total_slots = expert_size * mp_size * exp_loc * SLOT
    placement = (target[None, :] == jnp.arange(total_slots)[:, None]).astype(jnp.bfloat16)
    x_assign = jnp.repeat(x_rows, 2, axis=0)
    outgoing = jnp.dot(placement, x_assign, preferred_element_type=jnp.float32).astype(jnp.bfloat16)
    outgoing = outgoing.reshape(expert_size * mp_size, exp_loc * SLOT, width_loc)
    arrived = lax.all_to_all(outgoing, ("expert", "mp"), split_axis=0, concat_axis=2, tiled=True)
    expert_in = arrived.transpose(1, 0, 2)
    shard_piece = lax.all_gather(expert_in, ("leaf", "mp"), axis=0, tiled=True)
    gate_part = jnp.einsum("njd,jdf->njf", shard_piece, w_gate, preferred_element_type=jnp.float32)
    up_part = jnp.einsum("njd,jdf->njf", shard_piece, w_up, preferred_element_type=jnp.float32)
    units = (jax.nn.silu(gate_part) * up_part).astype(jnp.bfloat16)
    expert_out = lax.psum_scatter(
        jnp.einsum("njf,jfd->njd", units, w_down, preferred_element_type=jnp.float32),
        ("leaf", "mp"),
        scatter_dimension=0,
        tiled=True,
    ).astype(jnp.bfloat16)
    going_back = expert_out.transpose(1, 0, 2).reshape(
        1, exp_loc * SLOT, expert_size * mp_size, width_loc
    )
    returned = lax.all_to_all(going_back, ("expert", "mp"), split_axis=2, concat_axis=0, tiled=True)
    returned = returned.reshape(total_slots, width_loc)
    weight_rows = (
        (placement.astype(jnp.float32) * gate_values[None, :])
        .reshape(total_slots, row_count, 2)
        .sum(axis=2)
    )
    delta_rows = jnp.dot(
        weight_rows.T, returned.astype(jnp.float32), precision=lax.Precision.HIGHEST
    )
    mixed = (x_rows.astype(jnp.float32) + delta_rows).astype(jnp.bfloat16)
    return mixed.reshape(child_dev, steps_here, width_loc)


def solution(mesh):
    in_specs = (
        P("leaf", "expert", None, None, None),
        P("leaf", ("expert", "mp")),
        P(),
        P(),
        P("leaf", None, ("expert", "mp"), None),
        P("leaf", "expert", None, None, None),
        P("leaf", None, None),
        P("leaf", None, None),
        P("expert", None, ("leaf", "mp")),
        P("expert", None, ("leaf", "mp")),
        P("expert", ("leaf", "mp"), None),
    )
    out_specs = P("leaf", None, ("expert", "mp"))
    return jax.shard_map(local, mesh=mesh, in_specs=in_specs, out_specs=out_specs, check_vma=False)
```

profile of v0, /device:TPU:1, one launch (start us, length us, event | category | flops | bytes accessed | tf_op | source)
XLA Modules:
  0.0 751.7 jit_solution(13445200101908662211)
XLA Ops:
  6.5 0.0 copy-start
  6.5 0.0 all-gather.4.cloned.1.call-start
  6.5 0.7 all-gather.4.cloned.1.call-update
  7.3 0.0 all-gather.6.cloned.1.call-start
  7.3 0.7 compare_select_fusion.1
  8.1 1.3 gather_fusion
  9.4 74.7 %all-gather = bf16[32,1,384]{2,1,0:T(2,128)(2,1)S(1)} all-gather(bf16[1,1,384]{2,1,0:T(2,128)(2,1)} %bitcast.140), channel_id=1, replica_groups=mesh['leaf'=32,'expert'=8,'mp'=2] {'leaf'}, dimensions={0}, use_global_device_ids=true | all-gather | bytes 25344 | tf_op jit(solution)/shard_map/all_gather | solution.py:35
  84.0 0.7 and_select_fusion.5
  84.8 0.2 fusion.46
  85.0 0.8 copy.63
  85.7 0.1 eq.54
  85.9 0.2 convert_reduce_fusion
  86.1 0.7 slice_bitcast_fusion.2
  86.8 0.9 fusion.100
  87.7 0.0 copy-start.4
  87.7 30.5 %all-gather.4.cloned.1.call-done = bf16[32,1,2,256,128]{4,3,2,1,0:T(8,128)(2,1)} async-done(((bf16[1,1,2,256,128]{4,3,2,1,0:T(8,128)(2,1)}), bf16[32,1,2,256,128]{4,3,2,1,0:T(8,128)(2,1)}) %all-gather.4.cloned.1.call-update) | async-done | bytes 4194320 | tf_op jit(solution)/shard_map/all_gather | solution.py:34
  118.2 4.6 fusion.13
  122.8 0.0 copy-start.3
  122.8 0.2 slice_bitcast_fusion
  123.0 0.0 copy-done.4
  123.1 0.4 fusion.99
  123.4 0.2 fusion.70
  123.7 0.2 fusion.54
  123.9 0.2 fusion.42
  124.2 0.1 convolution_convert_fusion
  124.4 11.5 %all_to_all.30 = bf16[16,2,384]{2,1,0:T(2,128)(2,1)S(1)} all-to-all(bf16[16,2,384]{2,1,0:T(2,128)(2,1)S(1)} %reshape.149), channel_id=1, replica_groups=mesh['leaf'=32,'expert'=8,'mp'=2] {'expert','mp'}, dimensions={0} | all-to-all | bytes 49152 | tf_op jit(solution)/shard_map/all_to_all | solution.py:100
  135.9 0.7 copy.69
  136.5 0.0 all-gather.6.cloned.1.call-update
  136.6 0.1 reduce_sum.41
  136.6 0.1 copy.64
  136.7 0.0 copy-done.2
  136.7 0.1 mul.70
  136.8 0.0 copy-done.3
  136.8 0.1 mul.71
  136.9 1.3 dynamic-slice
  138.9 0.0 copy-start.1
  138.9 227.5 %all-gather.6.cloned.1.call-done = bf16[128,1,6144]{2,1,0:T(2,128)(2,1)} async-done(((bf16[2,1,6144]{2,1,0:T(2,128)(2,1)}), bf16[128,1,6144]{2,1,0:T(2,128)(2,1)}) %all-gather.6.cloned.1.call-update) | async-done | bytes 1572880 | tf_op jit(solution)/shard_map/all_gather | solution.py:102
  366.3 3.5 fusion.16
  369.8 0.0 copy-done
  369.8 0.0 copy-done.1
  369.8 5.2 convolution_bitcast_fusion
  375.0 261.2 %all-reduce.2 = bf16[128,1,6144]{2,0,1:T(8,128)(2,1)S(1)} all-reduce(f32[128,1,6144]{2,0,1:T(8,128)} %convolution_bitcast_fusion), channel_id=2, replica_groups=mesh['leaf'=32,'expert'=8,'mp'=2] {'leaf','mp'}, use_global_device_ids=true, to_apply=%region_6.9.clone | all-reduce | flops 786432 | bytes 4718592
  636.3 0.6 dynamic-slice_convert_fusion
  636.9 101.3 %all-to-all-start.1 = ((bf16[1,2,16,384]{3,1,0,2:T(2,128)(2,1)}), bf16[1,2,16,384]{3,1,0,2:T(2,128)(2,1)S(1)}, u32[]{:S(2)}, u32[]{:S(2)}) async-start(bf16[1,2,16,384]{3,1,0,2:T(2,128)(2,1)} %bitcast.34), calls=%async_computation.1 | async-start | bytes 49152 | tf_op jit(solution)/shard_map/all_to_all | solution.py:115
  738.3 0.1 multiply_reduce_fusion
  738.3 5.8 all-to-all-done.1
  744.1 0.1 fusion.45
  744.3 0.6 reshape.156
  (22 shorter events, 0.3 us)
Async XLA Ops:
  6.5 363.3 %copy-start = (bf16[1,128,6144]{2,1,0:T(8,128)(2,1)S(1)}, bf16[1,128,6144]{2,1,0:T(8,128)(2,1)}, u32[]{:S(2)}) copy-start(bf16[1,128,6144]{2,1,0:T(8,128)(2,1)} %param.25) | copy-start | bytes 4718596
  6.5 111.6 %all-gather.4.cloned.1.call-start = ((), (), s32[]{:S(2)}) async-start(), calls=%async_computation.2 | async-start | bytes 4325376 | tf_op jit(solution)/shard_map/all_gather | solution.py:34
  7.3 359.1 %all-gather.6.cloned.1.call-start = ((), (), s32[]{:S(2)}) async-start(), calls=%async_computation.3 | async-start | bytes 3194880 | tf_op jit(solution)/shard_map/all_gather | solution.py:102
  87.7 35.4 %copy-start.4 = (bf16[2,4,3,128]{3,1,2,0:T(4,128)(2,1)S(1)}, bf16[2,4,3,128]{3,1,2,0:T(4,128)(2,1)}, u32[]{:S(2)}) copy-start(bf16[2,4,3,128]{3,1,2,0:T(4,128)(2,1)} %param.19) | copy-start | bytes 18436
  122.8 13.9 %copy-start.2 = (s32[2,4,2]{1,2,0:T(2,128)S(1)}, s32[2,4,2]{1,2,0:T(2,128)}, u32[]{:S(2)}) copy-start(s32[2,4,2]{1,2,0:T(2,128)} %param.21) | copy-start | bytes 196
  122.8 14.0 %copy-start.3 = (f32[2,4,2]{1,2,0:T(2,128)S(1)}, f32[2,4,2]{1,2,0:T(2,128)}, u32[]{:S(2)}) copy-start(f32[2,4,2]{1,2,0:T(2,128)} %param.22) | copy-start | bytes 196
  138.9 231.0 %copy-start.1 = (bf16[1,6144,128]{2,1,0:T(8,128)(2,1)S(1)}, bf16[1,6144,128]{2,1,0:T(8,128)(2,1)}, u32[]{:S(2)}) copy-start(bf16[1,6144,128]{2,1,0:T(8,128)(2,1)} %param.24) | copy-start | bytes 4718596
  636.9 107.2 %all-to-all-start.1 = ((bf16[1,2,16,384]{3,1,0,2:T(2,128)(2,1)}), bf16[1,2,16,384]{3,1,0,2:T(2,128)(2,1)S(1)}, u32[]{:S(2)}, u32[]{:S(2)}) async-start(bf16[1,2,16,384]{3,1,0,2:T(2,128)(2,1)} %bitcast.34), calls=%async_computation.1 | async-start | bytes 49152 | tf_op jit(solution)/shard_map/all_to_all | solution.py:115
Sparse Core Ops, SparseCore 0:
  10.5 107.6 all-gather.3
  136.7 229.6 all-gather.5
where the time goes:
time: 752 us
  blocking collectives  347 us (46%)
  waiting for transfers between devices  264 us (35%)
  starting transfers between devices  101 us (13%)
  matrix products  15.5 us (2%)
  between operations  14.2 us (2%)
    unnamed x1, blocking collectives  261 us
    all_gather x1, waiting for transfers between devices, local(): shard_piece = lax.all_gather(expert_in, ('leaf', 'mp'), axis=0, tiled=True)  227 us
    all_to_all x1, starting transfers between devices, local(): lax.all_to_all(going_back, ('expert', 'mp'), split_axis=2, concat_axis=0,...  101 us
    all_gather x1, blocking collectives, local(): hidden_piece = lax.all_gather(node_hidden, 'leaf', axis=0, tiled=True)  74.7 us
    all_gather x1, waiting for transfers between devices, local(): cache_piece = lax.all_gather(node_cache, 'leaf', axis=0, tiled=True)  30.5 us
  transfers between devices with their start and end apart: 3, of which 3 were waited for; matrix products, arithmetic and copies ran while one was open for 1% of the time, Pallas kernels for 0%

commit v1 on v0

v1 whole, which is shorter than its diff:
```python
import functools

import jax
import jax.numpy as jnp
from jax import lax
from jax.experimental import pallas as pl
from jax.experimental.pallas import tpu as pltpu
from jax.sharding import PartitionSpec as P

F32 = jnp.float32
BF = jnp.bfloat16
SEMS = 256
LANES = 128
TOK = 8
HEADS = 3
NY = 8


class Ring:
    def __init__(self, size, me, device):
        self.size = size
        self.me = me
        self.device = device

    def at(self, offset):
        return lax.rem(self.me + offset + 2 * self.size, self.size)

    def right(self):
        return self.device(self.at(1))

    def left(self):
        return self.device(self.at(-1))


def interleave(jobs):
    jobs = list(jobs)
    while jobs:
        alive = []
        for job in jobs:
            try:
                next(job)
                alive.append(job)
            except StopIteration:
                pass
        jobs = alive


def kernel(
    geom,
    a_ref,
    b_ref,
    sel_ref,
    hid_ref,
    cache_ref,
    wg_ref,
    wu_ref,
    wd_ref,
    out_ref,
    scr,
):
    nx, ny, zh_n, zl_n = geom
    nz = zh_n * zl_n
    leaves = zh_n * ny
    tokens = leaves * TOK
    width = HEADS * LANES

    leaf = lax.axis_index("leaf")
    expert = lax.axis_index("expert")
    mp = lax.axis_index("mp")
    y = lax.rem(leaf, ny)
    zh = lax.div(leaf, ny)
    x = lax.div(expert, 2)
    core = lax.rem(expert, 2)
    z = zh * zl_n + mp

    def dev_x(k):
        return {"leaf": leaf, "expert": k * 2 + core, "mp": mp}

    def dev_y(k):
        return {"leaf": zh * ny + k, "expert": expert, "mp": mp}

    def dev_zh(k):
        return {"leaf": k * ny + y, "expert": expert, "mp": mp}

    def dev_z(k):
        return {
            "leaf": lax.div(k, zl_n) * ny + y,
            "expert": expert,
            "mp": lax.rem(k, zl_n),
        }

    sibling = {"leaf": leaf, "expert": x * 2 + (1 - core), "mp": mp}
    rx = Ring(nx, x, dev_x)
    ry = Ring(ny, y, dev_y)
    rz = Ring(nz, z, dev_z)
    rzh = Ring(zh_n, zh, dev_zh)

    send_sems, recv_sems, load_sems = scr["send"], scr["recv"], scr["load"]
    count = [0]
    sent = []

    def copy(src, dst, device):
        i = count[0]
        count[0] += 1
        c = pltpu.make_async_remote_copy(
            src_ref=src,
            dst_ref=dst,
            send_sem=send_sems.at[i],
            recv_sem=recv_sems.at[i],
            device_id=device,
            device_id_type=pl.DeviceIdType.MESH,
        )
        c.start()
        sent.append(c)
        return i

    def arrive(dst, i):
        pltpu.make_async_remote_copy(
            src_ref=dst,
            dst_ref=dst,
            send_sem=send_sems.at[i],
            recv_sem=recv_sems.at[i],
            device_id=sibling,
            device_id_type=pl.DeviceIdType.MESH,
        ).wait_recv()

    def gather(buf, ring, split, got=None):
        half = ring.size // 2
        right, left = ring.right(), ring.left()
        for s in range(1, half + 1):
            sp, sm = ring.at(1 - s), ring.at(s - 1)
            gp, gm = ring.at(-s), ring.at(s)
            if s < half:
                src_p, src_m = buf.at[sp], buf.at[sm]
                got_p, got_m = buf.at[gp], buf.at[gm]
            elif split:
                n = buf.shape[1] // 2
                src_p, src_m = buf.at[sp, pl.ds(0, n)], buf.at[sm, pl.ds(n, n)]
                got_p, got_m = buf.at[gp, pl.ds(0, n)], buf.at[gm, pl.ds(n, n)]
            else:
                src_p, src_m = buf.at[sp], None
                got_p, got_m = buf.at[gp], None
            ip = copy(src_p, src_p, right)
            if src_m is not None:
                im = copy(src_m, src_m, left)
            yield
            arrive(got_p, ip)
            if s == half and split:
                if got is not None:
                    n = buf.shape[1] // 2
                    got((gp, pl.ds(0, n)))
                arrive(got_m, im)
                if got is not None:
                    got((gm, pl.ds(n, n)))
            else:
                if got is not None:
                    got((gp,))
                if got_m is not None:
                    arrive(got_m, im)
                    if got is not None:
                        got((gm,))

    def add_into(ref, index, other, oindex):
        ref[index] = (ref[index].astype(F32) + other[oindex].astype(F32)).astype(BF)

    def scatter(h, rp, rm, ring, split, finish):
        half = ring.size // 2
        right, left = ring.right(), ring.left()
        n = h.shape[1] // 2
        lo, hi = pl.ds(0, n), pl.ds(n, n)
        for s in range(1, half + 1):
            dp, dm = ring.at(half - s + 1), ring.at(s - half - 1)
            if s == 1:
                if split:
                    ip = copy(h.at[dp, lo], rp.at[0, lo], right)
                    im = copy(h.at[dm, hi], rm.at[0, hi], left)
                else:
                    ip = copy(h.at[dp], rp.at[0], right)
                    im = None
            else:
                if s == 2:
                    if split:
                        add_into(rp, (0, lo), h, (dp, lo))
                        rp[0, hi] = h[dp, hi]
                        add_into(rm, (0, hi), h, (dm, hi))
                        rm[0, lo] = h[dm, lo]
                    else:
                        add_into(rp, 0, h, dp)
                else:
                    add_into(rp, s - 2, h, dp)
                    add_into(rm, s - 2, h, dm)
                ip = copy(rp.at[s - 2], rp.at[s - 1], right)
                if s == 2 and not split:
                    im = copy(h.at[dm], rm.at[1], left)
                else:
                    im = copy(rm.at[s - 2], rm.at[s - 1], left)
            yield
            if s == 1 and split:
                arrive(rp.at[0, lo], ip)
                arrive(rm.at[0, hi], im)
            else:
                arrive(rp.at[s - 1], ip)
                if im is not None:
                    arrive(rm.at[s - 1], im)
        me = ring.me
        if half > 1:
            finish(
                h[me].astype(F32)
                + rp[half - 1].astype(F32)
                + rm[half - 1].astype(F32)
            )
        elif split:
            first = h[me, lo].astype(F32) + rp[0, lo].astype(F32)
            second = h[me, hi].astype(F32) + rm[0, hi].astype(F32)
            finish(jnp.concatenate([first, second], axis=0))
        else:
            finish(h[me].astype(F32) + rp[0].astype(F32))

    loads = [
        pltpu.make_async_copy(wg_ref.at[0], scr["wgu"].at[:, pl.ds(0, LANES)], load_sems.at[0]),
        pltpu.make_async_copy(wu_ref.at[0], scr["wgu"].at[:, pl.ds(LANES, LANES)], load_sems.at[1]),
        pltpu.make_async_copy(wd_ref.at[0], scr["wd"], load_sems.at[2]),
    ]
    for c in loads:
        c.start()

    abuf, bbuf = scr["abuf"], scr["bbuf"]
    abuf[y, zh] = a_ref[...]
    bbuf[zh, y] = b_ref[...]

    barrier = pltpu.get_barrier_semaphore()
    partners = [sibling]
    for ring in (rx, ry, rz, rzh):
        partners += [ring.right(), ring.left()]
    for partner in partners:
        pl.semaphore_signal(barrier, inc=1, device_id=partner, device_id_type=pl.DeviceIdType.MESH)
    pl.semaphore_wait(barrier, len(partners))

    def gather_a():
        yield from gather(abuf.at[y], rzh, False)
        yield from gather(abuf, ry, True)

    def gather_b():
        yield from gather(bbuf.at[zh], ry, False)
        yield from gather(bbuf, rzh, True)

    interleave([gather_a(), gather_b()])

    def rows_a(k):
        return jnp.concatenate(
            [
                abuf[:, i, pl.ds(k * TOK, TOK)].astype(F32).reshape(ny * TOK, LANES)
                for i in range(zh_n)
            ],
            axis=0,
        )

    new_k = bbuf[:, :, pl.ds(0, TOK)].astype(F32).reshape(tokens, LANES).astype(BF)
    new_v = bbuf[:, :, pl.ds(TOK, TOK)].astype(F32).reshape(tokens, LANES).astype(BF)
    old_k = cache_ref[0]
    old_v = cache_ref[1]
    contract = (((1,), (1,)), ((), ()))
    row_id = lax.broadcasted_iota(jnp.int32, (tokens, tokens), 0)
    col_id = lax.broadcasted_iota(jnp.int32, (tokens, tokens), 1)
    allowed = (row_id // 4 == col_id // 4) & (col_id <= row_id)
    scale = 1.0 / LANES**0.5
    mine = sel_ref[...]
    xp = [scr["xp0"], scr["xp1"], scr["xp2"]]
    for p in range(HEADS):
        q = rows_a(p).astype(BF)
        s_old = lax.dot_general(q, old_k, contract, preferred_element_type=F32) * scale
        s_new = lax.dot_general(q, new_k, contract, preferred_element_type=F32) * scale
        s_new = jnp.where(allowed, s_new, -1e30)
        top = jnp.maximum(
            jnp.max(s_old, axis=1, keepdims=True), jnp.max(s_new, axis=1, keepdims=True)
        )
        e_old = jnp.exp(s_old - top)
        e_new = jnp.exp(s_new - top)
        total = jnp.sum(e_old, axis=1, keepdims=True) + jnp.sum(e_new, axis=1, keepdims=True)
        inv = 1.0 / total
        attn = jnp.dot((e_old * inv).astype(BF), old_v, preferred_element_type=F32)
        attn += jnp.dot((e_new * inv).astype(BF), new_v, preferred_element_type=F32)
        row = hid_ref[:, pl.ds(p * LANES, LANES)].astype(F32)
        here = jnp.where(mine > 0.5, attn + row, 0.0)
        here = here.reshape(zh_n, ny, TOK, LANES)
        if p < 2:
            for i in range(zh_n):
                xp[p][:, i] = here[i].astype(BF)
        else:
            xp[p][...] = here.astype(BF)

    own = [scr["own0"], scr["own1"], scr["own2"]]
    rp = scr["xrp"]
    rm = scr["xrm"]
    mids = scr["xmid"]
    xs = scr["xs"]

    def own_at(p):
        if p == 0:
            return own[0].at[z, y]
        if p == 1:
            return own[1].at[x, z]
        return own[2].at[y, x]

    def home(p):
        first, second = (ry, rzh) if p < 2 else (rzh, ry)

        def keep(v):
            mids[p][...] = v.astype(BF)

        yield from scatter(xp[p], rp[p][0], rm[p][0], first, True, keep)

        def final(v):
            w = v.astype(BF)
            xs[p] = w
            if p == 0:
                own[0][z, y, x] = w
            elif p == 1:
                own[1][x, z, y] = w
            else:
                own[2][y, x, z] = w

        yield from scatter(mids[p], rp[p][1], rm[p][1], second, False, final)

    interleave([home(p) for p in range(HEADS)])

    sib = [scr["sib0"], scr["sib1"], scr["sib2"]]
    d2d = []
    orders = [(rx, ry, rz), (ry, rz, rx), (rz, rx, ry)]

    def everywhere(p):
        one, two, three = orders[p]
        yield from gather(own_at(p), one, False)
        last = own[p].at[three.me]
        yield from gather(last, two, True)

        def forward(index):
            i = copy(own[p].at[index], sib[p].at[index], sibling)
            d2d.append((sib[p].at[index], i))

        forward((three.me,))
        yield from gather(own[p], three, True, forward)

    interleave([everywhere(p) for p in range(HEADS)])

    def tiles(refs, p, xi, m, i):
        zi = i * zl_n + m
        if p == 0:
            return refs[0].at[zi, :, xi]
        if p == 1:
            return refs[1].at[xi, zi]
        return refs[2].at[:, xi, zi]

    acc = scr["acc"]
    acc[...] = jnp.zeros_like(acc)
    for c in loads:
        c.wait()
    blocks = nx * zl_n

    def up(refs, which):
        @pl.loop(0, blocks)
        def _(j):
            xi, m = lax.div(j, zl_n), lax.rem(j, zl_n)
            cols = []
            for p in range(HEADS):
                cols.append(
                    jnp.concatenate(
                        [
                            tiles(refs, p, xi, m, i)[...].astype(F32).reshape(ny * TOK, LANES)
                            for i in range(zh_n)
                        ],
                        axis=0,
                    ).astype(BF)
                )
            rows = jnp.concatenate(cols, axis=1)
            off = pl.multiple_of(((xi * 2 + which) * zl_n + m) * width, LANES)
            acc[...] += jnp.dot(rows, scr["wgu"][pl.ds(off, width), :], preferred_element_type=F32)

    up(own, core)
    for ref, i in d2d:
        arrive(ref, i)
    up(sib, 1 - core)

    gates = rows_a(HEADS)
    gate = gates[:, 0:1] + gates[:, 1:2]
    g = acc[:, pl.ds(0, LANES)]
    u = acc[:, pl.ds(LANES, LANES)]
    units = (g * (1.0 / (1.0 + jnp.exp(-g))) * u).astype(BF).astype(F32)
    scr["units"][...] = (units * gate).astype(BF)

    hs = [scr["hs0"], scr["hs1"], scr["hs2"]]
    ho = [scr["ho0"], scr["ho1"], scr["ho2"]]
    hr = [scr["hr0"], scr["hr1"], scr["hr2"]]

    def down(refs, which):
        @pl.loop(0, blocks)
        def _(j):
            xi, m = lax.div(j, zl_n), lax.rem(j, zl_n)
            off = pl.multiple_of(((xi * 2 + which) * zl_n + m) * width, LANES)
            o = jnp.dot(
                scr["units"][...], scr["wd"][:, pl.ds(off, width)], preferred_element_type=F32
            )
            for p in range(HEADS):
                part = o[:, p * LANES : (p + 1) * LANES].reshape(zh_n, ny, TOK, LANES)
                for i in range(zh_n):
                    tiles(refs, p, xi, m, i)[...] = part[i].astype(BF)

    down(hs, 1 - core)
    crossing = [copy(hs[p], hr[p], sibling) for p in range(HEADS)]
    down(ho, core)
    for p in range(HEADS):
        arrive(hr[p], crossing[p])

        @pl.loop(0, ho[p].shape[0])
        def _(k):
            add_into(ho[p], k, hr[p], k)

    grp, grm = scr["grp"], scr["grm"]
    gmid = scr["gmid"]

    def back(p):
        one, two, three = orders[p]

        def keep(level):
            def write(v):
                gmid[p][level][...] = v.astype(BF)

            return write

        yield from scatter(ho[p], grp[p][0], grm[p][0], three, True, keep(0))
        yield from scatter(gmid[p][0], grp[p][1], grm[p][1], two, True, keep(1))

        def final(v):
            out_ref[:, pl.ds(p * LANES, LANES)] = (xs[p].astype(F32) + v).astype(BF)

        yield from scatter(gmid[p][1], grp[p][2], grm[p][2], one, False, final)

    interleave([back(p) for p in range(HEADS)])

    for c in sent:
        c.wait_send()


def scratch_of(geom, features):
    nx, ny, zh_n, zl_n = geom
    nz = zh_n * zl_n
    tokens = zh_n * ny * TOK
    tile = (TOK, LANES)
    vm = lambda *shape: pltpu.VMEM(shape + tile, BF)
    full = [(nz, ny, nx), (nx, nz, ny), (ny, nx, nz)]
    scr = {
        "send": pltpu.SemaphoreType.DMA((SEMS,)),
        "recv": pltpu.SemaphoreType.DMA((SEMS,)),
        "load": pltpu.SemaphoreType.DMA((3,)),
        "wgu": pltpu.VMEM((features, 2 * LANES), BF),
        "wd": pltpu.VMEM((LANES, features), BF),
        "abuf": pltpu.VMEM((ny, zh_n, 32, LANES), BF),
        "bbuf": pltpu.VMEM((zh_n, ny, 16, LANES), BF),
        "xs": vm(HEADS),
        "acc": pltpu.VMEM((tokens, 2 * LANES), F32),
        "units": pltpu.VMEM((tokens, LANES), BF),
    }
    for p in range(HEADS):
        a, b, c = full[p]
        for name in ("own", "sib", "hs", "ho", "hr"):
            scr[name + str(p)] = vm(a, b, c)
        scr["xp" + str(p)] = vm(ny, zh_n) if p < 2 else vm(zh_n, ny)
    scr["xmid"] = [vm(zh_n), vm(zh_n), vm(ny)]
    halves = lambda n: max(n // 2, 1)
    scr["xrp"] = []
    scr["xrm"] = []
    scr["grp"] = []
    scr["grm"] = []
    scr["gmid"] = []
    for p in range(HEADS):
        first, second = (ny, zh_n) if p < 2 else (zh_n, ny)
        a, b, c = full[p]
        for key in ("xrp", "xrm"):
            scr[key].append([vm(halves(first), second), vm(halves(second))])
        for key in ("grp", "grm"):
            scr[key].append([vm(halves(a), b, c), vm(halves(b), c), vm(halves(c))])
        scr["gmid"].append([vm(b, c), vm(c)])
    return scr


def local(
    geom,
    node_cache,
    node_hidden,
    node_slot,
    parent,
    child_query,
    child_kv,
    routes,
    gate_w,
    w_gate,
    w_up,
    w_down,
):
    nx, ny, zh_n, zl_n = geom
    leaf = lax.axis_index("leaf")
    expert = lax.axis_index("expert")
    queries = child_query.reshape(TOK, HEADS, LANES).transpose(1, 0, 2).reshape(HEADS * TOK, LANES)
    weight = jnp.sum(jnp.where(routes == expert, gate_w, 0.0), axis=-1).reshape(TOK, 1)
    high = weight.astype(BF).astype(F32)
    lane = jnp.arange(LANES)[None, :]
    gates = jnp.where(lane == 0, high, jnp.where(lane == 1, weight - high, 0.0)).astype(BF)
    a = jnp.concatenate([queries, gates], axis=0)
    b = child_kv[:, 0].transpose(1, 0, 2, 3).reshape(2 * TOK, LANES)
    node = jnp.sum(jnp.where(node_slot == leaf, jnp.arange(node_slot.shape[0]), 0))
    mine = jnp.broadcast_to((parent == node).astype(F32)[:, None], (parent.shape[0], 4))
    mine = jnp.broadcast_to(mine.reshape(-1, 1), (parent.shape[0] * 4, LANES))
    features = w_gate.shape[1]
    vmem = pl.BlockSpec(memory_space=pltpu.VMEM)
    hbm = pl.BlockSpec(memory_space=pl.ANY)
    out = pl.pallas_call(
        functools.partial(kernel, geom),
        out_shape=jax.ShapeDtypeStruct((TOK, HEADS * LANES), BF),
        in_specs=[vmem] * 5 + [hbm] * 3,
        out_specs=vmem,
        scratch_shapes=[scratch_of(geom, features)],
        compiler_params=pltpu.CompilerParams(
            collective_id=0, has_side_effects=True, vmem_limit_bytes=58 * 1024 * 1024
        ),
    )(a, b, mine, node_hidden, node_cache[0, 0], w_gate, w_up, w_down)
    return out.reshape(child_query.shape[0], child_query.shape[1], HEADS * LANES)


def solution(mesh):
    leaves, experts, mp = mesh.shape["leaf"], mesh.shape["expert"], mesh.shape["mp"]
    geom = (experts // 2, NY, leaves // NY, mp)
    in_specs = (
        P("leaf", "expert", None, None, None),
        P("leaf", ("expert", "mp")),
        P(),
        P(),
        P("leaf", None, ("expert", "mp"), None),
        P("leaf", "expert", None, None, None),
        P("leaf", None, None),
        P("leaf", None, None),
        P("expert", None, ("leaf", "mp")),
        P("expert", None, ("leaf", "mp")),
        P("expert", ("leaf", "mp"), None),
    )
    out_specs = P("leaf", None, ("expert", "mp"))
    return jax.shard_map(
        functools.partial(local, geom),
        mesh=mesh,
        in_specs=in_specs,
        out_specs=out_specs,
        check_vma=False,
    )
```

time: 752 us -> 150 us (0.20)
  the two profiles are of different devices: /device:TPU:1 before, /device:TPU:16 now
where the time goes in v1:
time: 150 us
  Pallas kernels  141 us (94%)
  local copies, waits for them, and re-layouts  4.28 us (3%)
  other arithmetic  4 us (3%)
    pallas_call x1, Pallas kernels, local(): pl.pallas_call(functools.partial(kernel, geom), out_shape=jax.ShapeDtypeS...  141 us

profile of v1, /device:TPU:16, one launch (start us, length us, event | category | flops | bytes accessed | tf_op | source)
XLA Modules:
  0.0 149.6 jit_solution(11545584212784061739)
XLA Ops:
  0.0 1.3 fusion.1
  1.3 1.3 compare_convert_fusion
  2.6 0.7 fusion
  3.3 0.1 reshape.49
  3.4 0.1 select_convert_fusion
  3.5 1.3 copy.14
  4.8 0.7 copy.13
  5.5 0.6 pad_maximum_fusion.a_ref
  6.1 0.1 broadcast_in_dim.65
  6.1 0.1 broadcast_in_dim.66
  6.2 0.7 broadcast_in_dim.67.sel_ref
  7.0 141.3 %shard_map.109 = bf16[8,384]{1,0:T(8,128)(2,1)} custom-call(bf16[32,128]{1,0:T(8,128)(2,1)} %pad_maximum_fusion.a_ref, bf16[16,128]{1,0:T(8,128)(2,1)} %bitcast.12, f32[256,128]{1,0:T(8,128)} %broadcast_in_dim.67.sel_ref, bf16[1,384]{1,0:T(2,128)(2,1)} %hid_ref.1, bf16[2,256,128]{2,1,0:T(8,128)(2,1)} %bitcast.10, bf16[1,6144,128]{2,1,0:T(8,128)(2,1)} %wg_ref.1, ...), custom_call_target="tpu_custom_call" | custom-call | tf_op jit(solution)/shard_map/pallas_call | solution.py:516
  148.3 1.3 reshape.51
  (3 shorter events, 0.0 us)

commit v2 on v1

--- a/solution.py
+++ b/solution.py
@@ -25,11 +25,11 @@
     def at(self, offset):
         return lax.rem(self.me + offset + 2 * self.size, self.size)
 
-    def right(self):
-        return self.device(self.at(1))
-
-    def left(self):
-        return self.device(self.at(-1))
+    def near_first(self):
+        return sorted(range(1, self.size), key=lambda k: (min(k, self.size - k), k))
+
+    def far_first(self):
+        return self.near_first()[::-1]
 
 
 def interleave(jobs):
@@ -47,9 +47,12 @@
 
 def kernel(
     geom,
-    a_ref,
-    b_ref,
-    sel_ref,
+    slot_ref,
+    routes_ref,
+    gate_ref,
+    parent_ref,
+    query_ref,
+    kv_ref,
     hid_ref,
     cache_ref,
     wg_ref,
@@ -124,125 +127,78 @@
             device_id_type=pl.DeviceIdType.MESH,
         ).wait_recv()
 
-    def gather(buf, ring, split, got=None):
-        half = ring.size // 2
-        right, left = ring.right(), ring.left()
-        for s in range(1, half + 1):
-            sp, sm = ring.at(1 - s), ring.at(s - 1)
-            gp, gm = ring.at(-s), ring.at(s)
-            if s < half:
-                src_p, src_m = buf.at[sp], buf.at[sm]
-                got_p, got_m = buf.at[gp], buf.at[gm]
-            elif split:
-                n = buf.shape[1] // 2
-                src_p, src_m = buf.at[sp, pl.ds(0, n)], buf.at[sm, pl.ds(n, n)]
-                got_p, got_m = buf.at[gp, pl.ds(0, n)], buf.at[gm, pl.ds(n, n)]
-            else:
-                src_p, src_m = buf.at[sp], None
-                got_p, got_m = buf.at[gp], None
-            ip = copy(src_p, src_p, right)
-            if src_m is not None:
-                im = copy(src_m, src_m, left)
-            yield
-            arrive(got_p, ip)
-            if s == half and split:
-                if got is not None:
-                    n = buf.shape[1] // 2
-                    got((gp, pl.ds(0, n)))
-                arrive(got_m, im)
-                if got is not None:
-                    got((gm, pl.ds(n, n)))
-            else:
-                if got is not None:
-                    got((gp,))
-                if got_m is not None:
-                    arrive(got_m, im)
-                    if got is not None:
-                        got((gm,))
+    def gather(buf, ring, got=None):
+        ids = {}
+        for k in ring.far_first():
+            ids[k] = copy(buf.at[ring.me], buf.at[ring.me], ring.device(ring.at(k)))
+        yield
+        for k in ring.near_first():
+            index = ring.at(-k)
+            arrive(buf.at[index], ids[k])
+            if got is not None:
+                got(index)
 
     def add_into(ref, index, other, oindex):
         ref[index] = (ref[index].astype(F32) + other[oindex].astype(F32)).astype(BF)
 
-    def scatter(h, rp, rm, ring, split, finish):
-        half = ring.size // 2
-        right, left = ring.right(), ring.left()
-        n = h.shape[1] // 2
-        lo, hi = pl.ds(0, n), pl.ds(n, n)
-        for s in range(1, half + 1):
-            dp, dm = ring.at(half - s + 1), ring.at(s - half - 1)
-            if s == 1:
-                if split:
-                    ip = copy(h.at[dp, lo], rp.at[0, lo], right)
-                    im = copy(h.at[dm, hi], rm.at[0, hi], left)
-                else:
-                    ip = copy(h.at[dp], rp.at[0], right)
-                    im = None
-            else:
-                if s == 2:
-                    if split:
-                        add_into(rp, (0, lo), h, (dp, lo))
-                        rp[0, hi] = h[dp, hi]
-                        add_into(rm, (0, hi), h, (dm, hi))
-                        rm[0, lo] = h[dm, lo]
-                    else:
-                        add_into(rp, 0, h, dp)
-                else:
-                    add_into(rp, s - 2, h, dp)
-                    add_into(rm, s - 2, h, dm)
-                ip = copy(rp.at[s - 2], rp.at[s - 1], right)
-                if s == 2 and not split:
-                    im = copy(h.at[dm], rm.at[1], left)
-                else:
-                    im = copy(rm.at[s - 2], rm.at[s - 1], left)
-            yield
-            if s == 1 and split:
-                arrive(rp.at[0, lo], ip)
-                arrive(rm.at[0, hi], im)
-            else:
-                arrive(rp.at[s - 1], ip)
-                if im is not None:
-                    arrive(rm.at[s - 1], im)
-        me = ring.me
-        if half > 1:
-            finish(
-                h[me].astype(F32)
-                + rp[half - 1].astype(F32)
-                + rm[half - 1].astype(F32)
-            )
-        elif split:
-            first = h[me, lo].astype(F32) + rp[0, lo].astype(F32)
-            second = h[me, hi].astype(F32) + rm[0, hi].astype(F32)
-            finish(jnp.concatenate([first, second], axis=0))
-        else:
-            finish(h[me].astype(F32) + rp[0].astype(F32))
+    def scatter(h, r, ring, finish):
+        ids = {}
+        for k in ring.far_first():
+            ids[k] = copy(h.at[ring.at(k)], r.at[k - 1], ring.device(ring.at(k)))
+        yield
+        total = h[ring.me].astype(F32)
+        for k in ring.near_first():
+            arrive(r.at[k - 1], ids[k])
+            total = total + r[k - 1].astype(F32)
+        finish(total)
 
     loads = [
         pltpu.make_async_copy(wg_ref.at[0], scr["wgu"].at[:, pl.ds(0, LANES)], load_sems.at[0]),
         pltpu.make_async_copy(wu_ref.at[0], scr["wgu"].at[:, pl.ds(LANES, LANES)], load_sems.at[1]),
         pltpu.make_async_copy(wd_ref.at[0], scr["wd"], load_sems.at[2]),
+        pltpu.make_async_copy(cache_ref.at[0, 0], scr["cache"], load_sems.at[3]),
     ]
     for c in loads:
         c.start()
 
     abuf, bbuf = scr["abuf"], scr["bbuf"]
-    abuf[y, zh] = a_ref[...]
-    bbuf[zh, y] = b_ref[...]
+    row = lax.broadcasted_iota(jnp.int32, (TOK, LANES), 0)
+    lane = lax.broadcasted_iota(jnp.int32, (TOK, LANES), 1)
+    weight = jnp.zeros((TOK, LANES), F32)
+    for t in range(TOK):
+        w = jnp.float32(0.0)
+        for k in range(2):
+            w += jnp.where(
+                routes_ref[t // 4, k, t % 4] == expert, gate_ref[t // 4, k, t % 4], 0.0
+            )
+        weight = jnp.where(row == t, w, weight)
+    high = weight.astype(BF).astype(F32)
+    for h in range(HEADS):
+        abuf[y, zh, pl.ds(h * TOK, TOK)] = (
+            query_ref[:, h].astype(F32).reshape(TOK, LANES).astype(BF)
+        )
+    abuf[y, zh, pl.ds(HEADS * TOK, TOK)] = jnp.where(
+        lane == 0, high, jnp.where(lane == 1, weight - high, 0.0)
+    ).astype(BF)
+    for k in range(2):
+        part = kv_ref[:, 0, k].astype(F32).reshape(TOK, LANES)
+        bbuf[zh, y, pl.ds(k * TOK, TOK)] = part.astype(BF)
 
     barrier = pltpu.get_barrier_semaphore()
     partners = [sibling]
-    for ring in (rx, ry, rz, rzh):
-        partners += [ring.right(), ring.left()]
+    for ring in (rx, ry, rz):
+        partners += [ring.device(ring.at(k)) for k in range(1, ring.size)]
     for partner in partners:
         pl.semaphore_signal(barrier, inc=1, device_id=partner, device_id_type=pl.DeviceIdType.MESH)
     pl.semaphore_wait(barrier, len(partners))
 
     def gather_a():
-        yield from gather(abuf.at[y], rzh, False)
-        yield from gather(abuf, ry, True)
+        yield from gather(abuf.at[y], rzh)
+        yield from gather(abuf, ry)
 
     def gather_b():
-        yield from gather(bbuf.at[zh], ry, False)
-        yield from gather(bbuf, rzh, True)
+        yield from gather(bbuf.at[zh], ry)
+        yield from gather(bbuf, rzh)
 
     interleave([gather_a(), gather_b()])
 
@@ -257,14 +213,22 @@
 
     new_k = bbuf[:, :, pl.ds(0, TOK)].astype(F32).reshape(tokens, LANES).astype(BF)
     new_v = bbuf[:, :, pl.ds(TOK, TOK)].astype(F32).reshape(tokens, LANES).astype(BF)
-    old_k = cache_ref[0]
-    old_v = cache_ref[1]
+    loads[3].wait()
+    old_k = scr["cache"][0]
+    old_v = scr["cache"][1]
     contract = (((1,), (1,)), ((), ()))
     row_id = lax.broadcasted_iota(jnp.int32, (tokens, tokens), 0)
     col_id = lax.broadcasted_iota(jnp.int32, (tokens, tokens), 1)
     allowed = (row_id // 4 == col_id // 4) & (col_id <= row_id)
     scale = 1.0 / LANES**0.5
-    mine = sel_ref[...]
+    node = jnp.int32(0)
+    for k in range(leaves):
+        node += jnp.where(slot_ref[k] == leaf, k, 0)
+    children = leaves * 2
+    token_child = lax.broadcasted_iota(jnp.int32, (tokens, children), 0) // 4
+    child_id = lax.broadcasted_iota(jnp.int32, (tokens, children), 1)
+    here_row = (token_child == child_id) & (parent_ref[...] == node)
+    mine = jnp.sum(jnp.where(here_row, 1.0, 0.0), axis=1, keepdims=True)
     xp = [scr["xp0"], scr["xp1"], scr["xp2"]]
     for p in range(HEADS):
         q = rows_a(p).astype(BF)
@@ -290,8 +254,7 @@
             xp[p][...] = here.astype(BF)
 
     own = [scr["own0"], scr["own1"], scr["own2"]]
-    rp = scr["xrp"]
-    rm = scr["xrm"]
+    xr = scr["xr"]
     mids = scr["xmid"]
     xs = scr["xs"]
 
@@ -308,7 +271,7 @@
         def keep(v):
             mids[p][...] = v.astype(BF)
 
-        yield from scatter(xp[p], rp[p][0], rm[p][0], first, True, keep)
+        yield from scatter(xp[p], xr[p][0], first, keep)
 
         def final(v):
             w = v.astype(BF)
@@ -320,7 +283,7 @@
             else:
                 own[2][y, x, z] = w
 
-        yield from scatter(mids[p], rp[p][1], rm[p][1], second, False, final)
+        yield from scatter(mids[p], xr[p][1], second, final)
 
     interleave([home(p) for p in range(HEADS)])
 
@@ -330,16 +293,16 @@
 
     def everywhere(p):
         one, two, three = orders[p]
-        yield from gather(own_at(p), one, False)
+        yield from gather(own_at(p), one)
         last = own[p].at[three.me]
-        yield from gather(last, two, True)
+        yield from gather(last, two)
 
         def forward(index):
             i = copy(own[p].at[index], sib[p].at[index], sibling)
             d2d.append((sib[p].at[index], i))
 
-        forward((three.me,))
-        yield from gather(own[p], three, True, forward)
+        forward(three.me)
+        yield from gather(own[p], three, forward)
 
     interleave([everywhere(p) for p in range(HEADS)])
 
@@ -353,7 +316,7 @@
 
     acc = scr["acc"]
     acc[...] = jnp.zeros_like(acc)
-    for c in loads:
+    for c in loads[:3]:
         c.wait()
     blocks = nx * zl_n
 
@@ -415,7 +378,7 @@
         def _(k):
             add_into(ho[p], k, hr[p], k)
 
-    grp, grm = scr["grp"], scr["grm"]
+    gr = scr["gr"]
     gmid = scr["gmid"]
 
     def back(p):
@@ -427,13 +390,15 @@
 
             return write
 
-        yield from scatter(ho[p], grp[p][0], grm[p][0], three, True, keep(0))
-        yield from scatter(gmid[p][0], grp[p][1], grm[p][1], two, True, keep(1))
+        yield from scatter(ho[p], gr[p][0], three, keep(0))
+        yield from scatter(gmid[p][0], gr[p][1], two, keep(1))
 
         def final(v):
-            out_ref[:, pl.ds(p * LANES, LANES)] = (xs[p].astype(F32) + v).astype(BF)
-
-        yield from scatter(gmid[p][1], grp[p][2], grm[p][2], one, False, final)
+            w = (xs[p].astype(F32) + v).astype(BF)
+            for c in range(2):
+                out_ref[c, :, pl.ds(p * LANES, LANES)] = w[c * 4 : c * 4 + 4]
+
+        yield from scatter(gmid[p][1], gr[p][2], one, final)
 
     interleave([back(p) for p in range(HEADS)])
 
@@ -451,7 +416,8 @@
     scr = {
         "send": pltpu.SemaphoreType.DMA((SEMS,)),
         "recv": pltpu.SemaphoreType.DMA((SEMS,)),
-        "load": pltpu.SemaphoreType.DMA((3,)),
+        "load": pltpu.SemaphoreType.DMA((4,)),
+        "cache": pltpu.VMEM((2, 256, LANES), BF),
         "wgu": pltpu.VMEM((features, 2 * LANES), BF),
         "wd": pltpu.VMEM((LANES, features), BF),
         "abuf": pltpu.VMEM((ny, zh_n, 32, LANES), BF),
@@ -466,19 +432,14 @@
             scr[name + str(p)] = vm(a, b, c)
         scr["xp" + str(p)] = vm(ny, zh_n) if p < 2 else vm(zh_n, ny)
     scr["xmid"] = [vm(zh_n), vm(zh_n), vm(ny)]
-    halves = lambda n: max(n // 2, 1)
-    scr["xrp"] = []
-    scr["xrm"] = []
-    scr["grp"] = []
-    scr["grm"] = []
+    scr["xr"] = []
+    scr["gr"] = []
     scr["gmid"] = []
     for p in range(HEADS):
         first, second = (ny, zh_n) if p < 2 else (zh_n, ny)
         a, b, c = full[p]
-        for key in ("xrp", "xrm"):
-            scr[key].append([vm(halves(first), second), vm(halves(second))])
-        for key in ("grp", "grm"):
-            scr[key].append([vm(halves(a), b, c), vm(halves(b), c), vm(halves(c))])
+        scr["xr"].append([vm(first - 1, second), vm(second - 1)])
+        scr["gr"].append([vm(a - 1, b, c), vm(b - 1, c), vm(c - 1)])
         scr["gmid"].append([vm(b, c), vm(c)])
     return scr
 
@@ -497,33 +458,32 @@
     w_up,
     w_down,
 ):
-    nx, ny, zh_n, zl_n = geom
-    leaf = lax.axis_index("leaf")
-    expert = lax.axis_index("expert")
-    queries = child_query.reshape(TOK, HEADS, LANES).transpose(1, 0, 2).reshape(HEADS * TOK, LANES)
-    weight = jnp.sum(jnp.where(routes == expert, gate_w, 0.0), axis=-1).reshape(TOK, 1)
-    high = weight.astype(BF).astype(F32)
-    lane = jnp.arange(LANES)[None, :]
-    gates = jnp.where(lane == 0, high, jnp.where(lane == 1, weight - high, 0.0)).astype(BF)
-    a = jnp.concatenate([queries, gates], axis=0)
-    b = child_kv[:, 0].transpose(1, 0, 2, 3).reshape(2 * TOK, LANES)
-    node = jnp.sum(jnp.where(node_slot == leaf, jnp.arange(node_slot.shape[0]), 0))
-    mine = jnp.broadcast_to((parent == node).astype(F32)[:, None], (parent.shape[0], 4))
-    mine = jnp.broadcast_to(mine.reshape(-1, 1), (parent.shape[0] * 4, LANES))
     features = w_gate.shape[1]
+    smem = pl.BlockSpec(memory_space=pltpu.SMEM)
     vmem = pl.BlockSpec(memory_space=pltpu.VMEM)
     hbm = pl.BlockSpec(memory_space=pl.ANY)
-    out = pl.pallas_call(
+    return pl.pallas_call(
         functools.partial(kernel, geom),
-        out_shape=jax.ShapeDtypeStruct((TOK, HEADS * LANES), BF),
-        in_specs=[vmem] * 5 + [hbm] * 3,
+        out_shape=jax.ShapeDtypeStruct(child_query.shape[:2] + (HEADS * LANES,), BF),
+        in_specs=[smem] * 3 + [vmem] * 4 + [hbm] * 4,
         out_specs=vmem,
         scratch_shapes=[scratch_of(geom, features)],
         compiler_params=pltpu.CompilerParams(
             collective_id=0, has_side_effects=True, vmem_limit_bytes=58 * 1024 * 1024
         ),
-    )(a, b, mine, node_hidden, node_cache[0, 0], w_gate, w_up, w_down)
-    return out.reshape(child_query.shape[0], child_query.shape[1], HEADS * LANES)
+    )(
+        node_slot,
+        routes.transpose(0, 2, 1),
+        gate_w.transpose(0, 2, 1),
+        parent.reshape(1, -1),
+        child_query.transpose(0, 2, 1, 3),
+        child_kv,
+        node_hidden,
+        node_cache,
+        w_gate,
+        w_up,
+        w_down,
+    )
 
 
 def solution(mesh):

time: 150 us -> 98.7 us (0.66)
  the two profiles are of different devices: /device:TPU:16 before, /device:TPU:1 now
where the time goes in v2:
time: 98.7 us; the launch traced here: 97.6 us
  Pallas kernels  96.3 us (98%)
  local copies, waits for them, and re-layouts  1.29 us (1%)
    pallas_call x1, Pallas kernels, local(): pl.pallas_call(functools.partial(kernel, geom), out_shape=jax.ShapeDtypeS...  96.3 us

profile of v2, /device:TPU:1, one launch (start us, length us, event | category | flops | bytes accessed | tf_op | source)
XLA Modules:
  0.0 97.6 jit_solution(9899819159460291031)
XLA Ops:
  0.0 96.3 %shard_map.109 = bf16[2,4,384]{2,1,0:T(4,128)(2,1)} custom-call(s32[32]{0:T(128)} %slot_ref.1, s32[2,2,4]{2,1,0:T(2,128)} %bitcast.5, f32[2,2,4]{2,1,0:T(2,128)} %bitcast.6, s32[1,64]{1,0:T(1,128)} %bitcast.7, bf16[2,3,4,128]{3,2,1,0:T(4,128)(2,1)} %bitcast.4, bf16[2,1,2,4,128]{4,3,2,1,0:T(4,128)(2,1)} %kv_ref.1, bf16[1,384]{1,0:T(2,128)(2,1)} %hid_ref.1, ...), custom_call_target="tpu_custom_call" | custom-call | tf_op jit(solution)/shard_map/pallas_call | solution.py:465
  96.4 1.3 %copy.13 = bf16[2,4,384]{2,1,0:T(4,128)(2,1)} copy(bf16[2,4,384]{2,1,0:T(4,128)(2,1)} %shard_map.109) | data formatting | bytes 12288

commit v3 on v2

--- a/solution.py
+++ b/solution.py
@@ -1,4 +1,5 @@
 import functools
+import itertools
 
 import jax
 import jax.numpy as jnp
@@ -9,7 +10,8 @@
 
 F32 = jnp.float32
 BF = jnp.bfloat16
-SEMS = 256
+SENDS = 40
+RECVS = 56
 LANES = 128
 TOK = 8
 HEADS = 3
@@ -99,64 +101,78 @@
     rzh = Ring(zh_n, zh, dev_zh)
 
     send_sems, recv_sems, load_sems = scr["send"], scr["recv"], scr["load"]
-    count = [0]
-    sent = []
-
-    def copy(src, dst, device):
-        i = count[0]
-        count[0] += 1
-        c = pltpu.make_async_remote_copy(
+    next_send = itertools.count()
+    next_recv = itertools.count()
+    pending = []
+
+    def transfer(src, dst, device, send, recv):
+        return pltpu.make_async_remote_copy(
             src_ref=src,
             dst_ref=dst,
-            send_sem=send_sems.at[i],
-            recv_sem=recv_sems.at[i],
+            send_sem=send_sems.at[send],
+            recv_sem=recv_sems.at[recv],
             device_id=device,
             device_id_type=pl.DeviceIdType.MESH,
         )
-        c.start()
-        sent.append(c)
-        return i
-
-    def arrive(dst, i):
-        pltpu.make_async_remote_copy(
-            src_ref=dst,
-            dst_ref=dst,
-            send_sem=send_sems.at[i],
-            recv_sem=recv_sems.at[i],
-            device_id=sibling,
-            device_id_type=pl.DeviceIdType.MESH,
-        ).wait_recv()
+
+    def arrive(ref, recv):
+        transfer(ref, ref, sibling, 0, recv).wait_recv()
 
     def gather(buf, ring, got=None):
-        ids = {}
+        others = buf.at[pl.ds(0, ring.size - 1)]
+        send = next(next_send)
+        recvs = {k: next(next_recv) for k in range(1, ring.size if got else 2)}
         for k in ring.far_first():
-            ids[k] = copy(buf.at[ring.me], buf.at[ring.me], ring.device(ring.at(k)))
+            mine = buf.at[ring.me]
+            transfer(mine, mine, ring.device(ring.at(k)), send, recvs[k if got else 1]).start()
+        pending.append((others, send))
         yield
-        for k in ring.near_first():
-            index = ring.at(-k)
-            arrive(buf.at[index], ids[k])
-            if got is not None:
+        if got is None:
+            arrive(others, recvs[1])
+        else:
+            for k in ring.near_first():
+                index = ring.at(-k)
+                arrive(buf.at[index], recvs[k])
                 got(index)
 
-    def add_into(ref, index, other, oindex):
-        ref[index] = (ref[index].astype(F32) + other[oindex].astype(F32)).astype(BF)
-
     def scatter(h, r, ring, finish):
-        ids = {}
+        send, recv = next(next_send), next(next_recv)
         for k in ring.far_first():
-            ids[k] = copy(h.at[ring.at(k)], r.at[k - 1], ring.device(ring.at(k)))
+            to = ring.at(k)
+            transfer(h.at[to], r.at[k - 1], ring.device(to), send, recv).start()
+        pending.append((r, send))
         yield
+        arrive(r, recv)
         total = h[ring.me].astype(F32)
-        for k in ring.near_first():
-            arrive(r.at[k - 1], ids[k])
-            total = total + r[k - 1].astype(F32)
+        for k in range(ring.size - 1):
+            total = total + r[k].astype(F32)
         finish(total)
+
+    barrier = pltpu.get_barrier_semaphore()
+    partners = [sibling]
+    for ring in (rx, ry, rz):
+        partners += [ring.device(ring.at(k)) for k in range(1, ring.size)]
+    for partner in partners:
+        pl.semaphore_signal(barrier, inc=1, device_id=partner, device_id_type=pl.DeviceIdType.MESH)
 
     loads = [
         pltpu.make_async_copy(wg_ref.at[0], scr["wgu"].at[:, pl.ds(0, LANES)], load_sems.at[0]),
         pltpu.make_async_copy(wu_ref.at[0], scr["wgu"].at[:, pl.ds(LANES, LANES)], load_sems.at[1]),
-        pltpu.make_async_copy(wd_ref.at[0], scr["wd"], load_sems.at[2]),
-        pltpu.make_async_copy(cache_ref.at[0, 0], scr["cache"], load_sems.at[3]),
+        pltpu.make_async_copy(cache_ref.at[0, 0], scr["cache"], load_sems.at[2]),
+    ]
+    span = zl_n * width
+
+    def down_block(i, which):
+        off = pl.multiple_of((i * 2 + which) * span, LANES)
+        return wd_ref.at[0, :, pl.ds(off, span)]
+
+    loads += [
+        pltpu.make_async_copy(
+            down_block(i, core),
+            scr["wd"].at[pl.ds(0, LANES), pl.ds(i * span, span)],
+            load_sems.at[3 + i],
+        )
+        for i in range(nx)
     ]
     for c in loads:
         c.start()
@@ -177,20 +193,22 @@
         abuf[y, zh, pl.ds(h * TOK, TOK)] = (
             query_ref[:, h].astype(F32).reshape(TOK, LANES).astype(BF)
         )
-    abuf[y, zh, pl.ds(HEADS * TOK, TOK)] = jnp.where(
+    bbuf[zh, y, pl.ds(2 * TOK, TOK)] = jnp.where(
         lane == 0, high, jnp.where(lane == 1, weight - high, 0.0)
     ).astype(BF)
     for k in range(2):
         part = kv_ref[:, 0, k].astype(F32).reshape(TOK, LANES)
         bbuf[zh, y, pl.ds(k * TOK, TOK)] = part.astype(BF)
 
-    barrier = pltpu.get_barrier_semaphore()
-    partners = [sibling]
-    for ring in (rx, ry, rz):
-        partners += [ring.device(ring.at(k)) for k in range(1, ring.size)]
-    for partner in partners:
-        pl.semaphore_signal(barrier, inc=1, device_id=partner, device_id_type=pl.DeviceIdType.MESH)
     pl.semaphore_wait(barrier, len(partners))
+
+    other = scr["wd"].at[pl.ds(LANES, LANES)]
+    wd_send, wd_recv = next(next_send), next(next_recv)
+    for i in range(nx):
+        transfer(
+            down_block(i, 1 - core), other.at[:, pl.ds(i * span, span)], sibling, wd_send, wd_recv
+        ).start()
+    pending.append((other, wd_send))
 
     def gather_a():
         yield from gather(abuf.at[y], rzh)
@@ -211,9 +229,12 @@
             axis=0,
         )
 
-    new_k = bbuf[:, :, pl.ds(0, TOK)].astype(F32).reshape(tokens, LANES).astype(BF)
-    new_v = bbuf[:, :, pl.ds(TOK, TOK)].astype(F32).reshape(tokens, LANES).astype(BF)
-    loads[3].wait()
+    def rows_b(k):
+        return bbuf[:, :, pl.ds(k * TOK, TOK)].astype(F32).reshape(tokens, LANES)
+
+    new_k = rows_b(0).astype(BF)
+    new_v = rows_b(1).astype(BF)
+    loads[2].wait()
     old_k = scr["cache"][0]
     old_v = scr["cache"][1]
     contract = (((1,), (1,)), ((), ()))
@@ -262,8 +283,8 @@
         if p == 0:
             return own[0].at[z, y]
         if p == 1:
-            return own[1].at[x, z]
-        return own[2].at[y, x]
+            return own[1].at[y, x]
+        return own[2].at[x, z]
 
     def home(p):
         first, second = (ry, rzh) if p < 2 else (rzh, ry)
@@ -279,9 +300,9 @@
             if p == 0:
                 own[0][z, y, x] = w
             elif p == 1:
-                own[1][x, z, y] = w
+                own[1][y, x, z] = w
             else:
-                own[2][y, x, z] = w
+                own[2][x, z, y] = w
 
         yield from scatter(mids[p], xr[p][1], second, final)
 
@@ -289,7 +310,7 @@
 
     sib = [scr["sib0"], scr["sib1"], scr["sib2"]]
     d2d = []
-    orders = [(rx, ry, rz), (ry, rz, rx), (rz, rx, ry)]
+    orders = [(rx, ry, rz), (rz, rx, ry), (ry, rz, rx)]
 
     def everywhere(p):
         one, two, three = orders[p]
@@ -297,10 +318,13 @@
         last = own[p].at[three.me]
         yield from gather(last, two)
 
+        send, recv = next(next_send), next(next_recv)
+
         def forward(index):
-            i = copy(own[p].at[index], sib[p].at[index], sibling)
-            d2d.append((sib[p].at[index], i))
-
+            transfer(own[p].at[index], sib[p].at[index], sibling, send, recv).start()
+
+        pending.append((own[p], send))
+        d2d.append((sib[p], recv))
         forward(three.me)
         yield from gather(own[p], three, forward)
 
@@ -311,12 +335,12 @@
         if p == 0:
             return refs[0].at[zi, :, xi]
         if p == 1:
-            return refs[1].at[xi, zi]
-        return refs[2].at[:, xi, zi]
+            return refs[1].at[:, xi, zi]
+        return refs[2].at[xi, zi]
 
     acc = scr["acc"]
     acc[...] = jnp.zeros_like(acc)
-    for c in loads[:3]:
+    for c in loads[:2] + loads[3:]:
         c.wait()
     blocks = nx * zl_n
 
@@ -340,49 +364,47 @@
             acc[...] += jnp.dot(rows, scr["wgu"][pl.ds(off, width), :], preferred_element_type=F32)
 
     up(own, core)
-    for ref, i in d2d:
-        arrive(ref, i)
+    for ref, recv in d2d:
+        arrive(ref, recv)
     up(sib, 1 - core)
 
-    gates = rows_a(HEADS)
+    gates = rows_b(2)
     gate = gates[:, 0:1] + gates[:, 1:2]
     g = acc[:, pl.ds(0, LANES)]
     u = acc[:, pl.ds(LANES, LANES)]
     units = (g * (1.0 / (1.0 + jnp.exp(-g))) * u).astype(BF).astype(F32)
-    scr["units"][...] = (units * gate).astype(BF)
-
-    hs = [scr["hs0"], scr["hs1"], scr["hs2"]]
+    mine_units, other_units = scr["units"], scr["units_other"]
+    mine_units[...] = (units * gate).astype(BF)
+    u_send, u_recv = next(next_send), next(next_recv)
+    transfer(mine_units, other_units, sibling, u_send, u_recv).start()
+    pending.append((other_units, u_send))
     ho = [scr["ho0"], scr["ho1"], scr["ho2"]]
-    hr = [scr["hr0"], scr["hr1"], scr["hr2"]]
-
-    def down(refs, which):
+    arrive(other, wd_recv)
+    arrive(other_units, u_recv)
+
+    def down(parts):
+        count = len(parts) * LANES
+
         @pl.loop(0, blocks)
         def _(j):
             xi, m = lax.div(j, zl_n), lax.rem(j, zl_n)
-            off = pl.multiple_of(((xi * 2 + which) * zl_n + m) * width, LANES)
-            o = jnp.dot(
-                scr["units"][...], scr["wd"][:, pl.ds(off, width)], preferred_element_type=F32
-            )
-            for p in range(HEADS):
-                part = o[:, p * LANES : (p + 1) * LANES].reshape(zh_n, ny, TOK, LANES)
+            both = jnp.concatenate([mine_units[...], other_units[...]], axis=1)
+            off = pl.multiple_of(j * width + parts[0] * LANES, LANES)
+            o = jnp.dot(both, scr["wd"][:, pl.ds(off, count)], preferred_element_type=F32)
+            for k, p in enumerate(parts):
+                part = o[:, k * LANES : (k + 1) * LANES].reshape(zh_n, ny, TOK, LANES)
                 for i in range(zh_n):
-                    tiles(refs, p, xi, m, i)[...] = part[i].astype(BF)
-
-    down(hs, 1 - core)
-    crossing = [copy(hs[p], hr[p], sibling) for p in range(HEADS)]
-    down(ho, core)
-    for p in range(HEADS):
-        arrive(hr[p], crossing[p])
-
-        @pl.loop(0, ho[p].shape[0])
-        def _(k):
-            add_into(ho[p], k, hr[p], k)
+                    tiles(ho, p, xi, m, i)[...] = part[i].astype(BF)
 
     gr = scr["gr"]
     gmid = scr["gmid"]
 
     def back(p):
         one, two, three = orders[p]
+        if p == 0:
+            down((0, 1))
+        if p == 2:
+            down((2,))
 
         def keep(level):
             def write(v):
@@ -402,8 +424,8 @@
 
     interleave([back(p) for p in range(HEADS)])
 
-    for c in sent:
-        c.wait_send()
+    for ref, send in pending:
+        transfer(ref, ref, sibling, send, 0).wait_send()
 
 
 def scratch_of(geom, features):
@@ -412,23 +434,24 @@
     tokens = zh_n * ny * TOK
     tile = (TOK, LANES)
     vm = lambda *shape: pltpu.VMEM(shape + tile, BF)
-    full = [(nz, ny, nx), (nx, nz, ny), (ny, nx, nz)]
+    full = [(nz, ny, nx), (ny, nx, nz), (nx, nz, ny)]
     scr = {
-        "send": pltpu.SemaphoreType.DMA((SEMS,)),
-        "recv": pltpu.SemaphoreType.DMA((SEMS,)),
-        "load": pltpu.SemaphoreType.DMA((4,)),
+        "send": pltpu.SemaphoreType.DMA((SENDS,)),
+        "recv": pltpu.SemaphoreType.DMA((RECVS,)),
+        "load": pltpu.SemaphoreType.DMA((3 + nx,)),
         "cache": pltpu.VMEM((2, 256, LANES), BF),
         "wgu": pltpu.VMEM((features, 2 * LANES), BF),
-        "wd": pltpu.VMEM((LANES, features), BF),
-        "abuf": pltpu.VMEM((ny, zh_n, 32, LANES), BF),
-        "bbuf": pltpu.VMEM((zh_n, ny, 16, LANES), BF),
+        "wd": pltpu.VMEM((2 * LANES, features // 2), BF),
+        "abuf": pltpu.VMEM((ny, zh_n, HEADS * TOK, LANES), BF),
+        "bbuf": pltpu.VMEM((zh_n, ny, 3 * TOK, LANES), BF),
         "xs": vm(HEADS),
         "acc": pltpu.VMEM((tokens, 2 * LANES), F32),
         "units": pltpu.VMEM((tokens, LANES), BF),
+        "units_other": pltpu.VMEM((tokens, LANES), BF),
     }
     for p in range(HEADS):
         a, b, c = full[p]
-        for name in ("own", "sib", "hs", "ho", "hr"):
+        for name in ("own", "sib", "ho"):
             scr[name + str(p)] = vm(a, b, c)
         scr["xp" + str(p)] = vm(ny, zh_n) if p < 2 else vm(zh_n, ny)
     scr["xmid"] = [vm(zh_n), vm(zh_n), vm(ny)]

time: 98.7 us -> 90.9 us (0.921)
  Pallas kernels: 96.3 us -> 89.4 us
    pallas_call x1, Pallas kernels: 96.3 us -> 89.4 us  [local(): pl.pallas_call(functools.partial(kernel, geom), out_shape=jax.ShapeDtypeS...]
where the time goes in v3:
time: 90.9 us; the launch traced here: 90.7 us
  Pallas kernels  89.4 us (98%)
  local copies, waits for them, and re-layouts  1.29 us (1%)
    pallas_call x1, Pallas kernels, local(): pl.pallas_call(functools.partial(kernel, geom), out_shape=jax.ShapeDtypeS...  89.4 us

profile of v3, /device:TPU:1, one launch (start us, length us, event | category | flops | bytes accessed | tf_op | source)
XLA Modules:
  0.0 90.7 jit_solution(9455563994866124901)
XLA Ops:
  0.0 89.4 %shard_map.109 = bf16[2,4,384]{2,1,0:T(4,128)(2,1)} custom-call(s32[32]{0:T(128)} %slot_ref.1, s32[2,2,4]{2,1,0:T(2,128)} %bitcast.5, f32[2,2,4]{2,1,0:T(2,128)} %bitcast.6, s32[1,64]{1,0:T(1,128)} %bitcast.7, bf16[2,3,4,128]{3,2,1,0:T(4,128)(2,1)} %bitcast.4, bf16[2,1,2,4,128]{4,3,2,1,0:T(4,128)(2,1)} %kv_ref.1, bf16[1,384]{1,0:T(2,128)(2,1)} %hid_ref.1, ...), custom_call_target="tpu_custom_call" | custom-call | tf_op jit(solution)/shard_map/pallas_call | solution.py:488
  89.4 1.3 %copy.13 = bf16[2,4,384]{2,1,0:T(4,128)(2,1)} copy(bf16[2,4,384]{2,1,0:T(4,128)(2,1)} %shard_map.109) | data formatting | bytes 12288

commit v4 on v3

--- a/solution.py
+++ b/solution.py
@@ -10,8 +10,8 @@
 
 F32 = jnp.float32
 BF = jnp.bfloat16
-SENDS = 40
-RECVS = 56
+SENDS = 44
+RECVS = 62
 LANES = 128
 TOK = 8
 HEADS = 3
@@ -65,6 +65,7 @@
 ):
     nx, ny, zh_n, zl_n = geom
     nz = zh_n * zl_n
+    cut_y, cut_z = cuts_of(geom)
     leaves = zh_n * ny
     tokens = leaves * TOK
     width = HEADS * LANES
@@ -148,6 +149,15 @@
             total = total + r[k].astype(F32)
         finish(total)
 
+    inputs = [slot_ref, routes_ref, gate_ref, parent_ref, query_ref, kv_ref, hid_ref]
+    held = scr["held"]
+    small = [
+        pltpu.make_async_copy(src, dst, scr["small"].at[i])
+        for i, (src, dst) in enumerate(zip(inputs, held))
+    ]
+    for c in small:
+        c.start()
+
     barrier = pltpu.get_barrier_semaphore()
     partners = [sibling]
     for ring in (rx, ry, rz):
@@ -177,6 +187,9 @@
     for c in loads:
         c.start()
 
+    for c in small:
+        c.wait()
+    slot_ref, routes_ref, gate_ref, parent_ref, query_ref, kv_ref, hid_ref = held
     abuf, bbuf = scr["abuf"], scr["bbuf"]
     row = lax.broadcasted_iota(jnp.int32, (TOK, LANES), 0)
     lane = lax.broadcasted_iota(jnp.int32, (TOK, LANES), 1)
@@ -274,17 +287,12 @@
         else:
             xp[p][...] = here.astype(BF)
 
-    own = [scr["own0"], scr["own1"], scr["own2"]]
+    own = scr["own"]
+    start = scr["start"]
     xr = scr["xr"]
     mids = scr["xmid"]
     xs = scr["xs"]
-
-    def own_at(p):
-        if p == 0:
-            return own[0].at[z, y]
-        if p == 1:
-            return own[1].at[y, x]
-        return own[2].at[x, z]
+    firsts = (ry, rz, ry)
 
     def home(p):
         first, second = (ry, rzh) if p < 2 else (rzh, ry)
@@ -297,46 +305,51 @@
         def final(v):
             w = v.astype(BF)
             xs[p] = w
-            if p == 0:
-                own[0][z, y, x] = w
-            elif p == 1:
-                own[1][y, x, z] = w
-            else:
-                own[2][x, z, y] = w
+            start[p][firsts[p].me] = w
 
         yield from scatter(mids[p], xr[p][1], second, final)
 
     interleave([home(p) for p in range(HEADS)])
 
-    sib = [scr["sib0"], scr["sib1"], scr["sib2"]]
+    sib = scr["sib"]
     d2d = []
-    orders = [(rx, ry, rz), (rz, rx, ry), (ry, rz, rx)]
-
-    def everywhere(p):
-        one, two, three = orders[p]
-        yield from gather(own_at(p), one)
-        last = own[p].at[three.me]
-        yield from gather(last, two)
+    rings = {"x": rx, "y": ry, "z": rz}
+    pieces = pieces_of(geom)
+
+    interleave([gather(start[p], firsts[p]) for p in range(HEADS)])
+
+    def everywhere(k):
+        p, low, many, two, three = pieces[k]
+        two, three = rings[two], rings[three]
+        own[k][three.me, two.me] = start[p][pl.ds(low, many)]
+        yield from gather(own[k].at[three.me], two)
 
         send, recv = next(next_send), next(next_recv)
 
         def forward(index):
-            transfer(own[p].at[index], sib[p].at[index], sibling, send, recv).start()
-
-        pending.append((own[p], send))
-        d2d.append((sib[p], recv))
+            transfer(own[k].at[index], sib[k].at[index], sibling, send, recv).start()
+
+        pending.append((own[k], send))
+        d2d.append((sib[k], recv))
         forward(three.me)
-        yield from gather(own[p], three, forward)
-
-    interleave([everywhere(p) for p in range(HEADS)])
+        yield from gather(own[k], three, forward)
+
+    interleave([everywhere(k) for k in range(len(pieces))])
 
     def tiles(refs, p, xi, m, i):
         zi = i * zl_n + m
         if p == 0:
-            return refs[0].at[zi, :, xi]
+            return [(refs[0].at[zi, xi], 0, cut_y), (refs[1].at[xi, zi], cut_y, ny - cut_y)]
         if p == 1:
-            return refs[1].at[:, xi, zi]
-        return refs[2].at[xi, zi]
+            if i * zl_n < cut_z:
+                return [(refs[2].at[:, xi, zi], 0, ny)]
+            return [(refs[3].at[xi, :, zi - cut_z], 0, ny)]
+        return [(refs[4].at[xi, zi], 0, ny)]
+
+    def rows_of(refs, p, xi, m, i):
+        parts = [ref[...].astype(F32) for ref, _, _ in tiles(refs, p, xi, m, i)]
+        part = parts[0] if len(parts) == 1 else jnp.concatenate(parts, axis=0)
+        return part.reshape(ny * TOK, LANES)
 
     acc = scr["acc"]
     acc[...] = jnp.zeros_like(acc)
@@ -352,10 +365,7 @@
             for p in range(HEADS):
                 cols.append(
                     jnp.concatenate(
-                        [
-                            tiles(refs, p, xi, m, i)[...].astype(F32).reshape(ny * TOK, LANES)
-                            for i in range(zh_n)
-                        ],
+                        [rows_of(refs, p, xi, m, i) for i in range(zh_n)],
                         axis=0,
                     ).astype(BF)
                 )
@@ -378,7 +388,7 @@
     u_send, u_recv = next(next_send), next(next_recv)
     transfer(mine_units, other_units, sibling, u_send, u_recv).start()
     pending.append((other_units, u_send))
-    ho = [scr["ho0"], scr["ho1"], scr["ho2"]]
+    ho = scr["ho"]
     arrive(other, wd_recv)
     arrive(other_units, u_recv)
 
@@ -394,50 +404,74 @@
             for k, p in enumerate(parts):
                 part = o[:, k * LANES : (k + 1) * LANES].reshape(zh_n, ny, TOK, LANES)
                 for i in range(zh_n):
-                    tiles(ho, p, xi, m, i)[...] = part[i].astype(BF)
-
-    gr = scr["gr"]
-    gmid = scr["gmid"]
-
-    def back(p):
-        one, two, three = orders[p]
-        if p == 0:
+                    for ref, low, many in tiles(ho, p, xi, m, i):
+                        ref[...] = part[i][low : low + many].astype(BF)
+
+    gr, gmid, ends, er = scr["gr"], scr["gmid"], scr["ends"], scr["er"]
+
+    def back(k):
+        p, low, many, two, three = pieces[k]
+        if k == 0:
             down((0, 1))
         if p == 2:
             down((2,))
 
-        def keep(level):
-            def write(v):
-                gmid[p][level][...] = v.astype(BF)
-
-            return write
-
-        yield from scatter(ho[p], gr[p][0], three, keep(0))
-        yield from scatter(gmid[p][0], gr[p][1], two, keep(1))
-
+        def keep(v):
+            gmid[k][...] = v.astype(BF)
+
+        def end(v):
+            ends[p][pl.ds(low, many)] = v.astype(BF)
+
+        yield from scatter(ho[k], gr[k][0], rings[three], keep)
+        yield from scatter(gmid[k], gr[k][1], rings[two], end)
+
+    interleave([back(k) for k in range(len(pieces))])
+
+    def last(p):
         def final(v):
             w = (xs[p].astype(F32) + v).astype(BF)
             for c in range(2):
                 out_ref[c, :, pl.ds(p * LANES, LANES)] = w[c * 4 : c * 4 + 4]
 
-        yield from scatter(gmid[p][1], gr[p][2], one, final)
-
-    interleave([back(p) for p in range(HEADS)])
+        yield from scatter(ends[p], er[p], firsts[p], final)
+
+    interleave([last(p) for p in range(HEADS)])
 
     for ref, send in pending:
         transfer(ref, ref, sibling, send, 0).wait_send()
 
 
-def scratch_of(geom, features):
+def cuts_of(geom):
+    nx, ny, zh_n, zl_n = geom
+    return ny * 3 // 4, zh_n * 3 // 4 * zl_n
+
+
+def pieces_of(geom):
+    nx, ny, zh_n, zl_n = geom
+    nz = zh_n * zl_n
+    cut_y, cut_z = cuts_of(geom)
+    return [
+        (0, 0, cut_y, "x", "z"),
+        (0, cut_y, ny - cut_y, "z", "x"),
+        (1, 0, cut_z, "x", "y"),
+        (1, cut_z, nz - cut_z, "y", "x"),
+        (2, 0, ny, "z", "x"),
+    ]
+
+
+def scratch_of(geom, features, held):
     nx, ny, zh_n, zl_n = geom
     nz = zh_n * zl_n
     tokens = zh_n * ny * TOK
     tile = (TOK, LANES)
     vm = lambda *shape: pltpu.VMEM(shape + tile, BF)
-    full = [(nz, ny, nx), (ny, nx, nz), (nx, nz, ny)]
+    size = {"x": nx, "y": ny, "z": nz}
+    pieces = pieces_of(geom)
     scr = {
         "send": pltpu.SemaphoreType.DMA((SENDS,)),
         "recv": pltpu.SemaphoreType.DMA((RECVS,)),
+        "held": held,
+        "small": pltpu.SemaphoreType.DMA((len(held),)),
         "load": pltpu.SemaphoreType.DMA((3 + nx,)),
         "cache": pltpu.VMEM((2, 256, LANES), BF),
         "wgu": pltpu.VMEM((features, 2 * LANES), BF),
@@ -450,20 +484,22 @@
         "units_other": pltpu.VMEM((tokens, LANES), BF),
     }
     for p in range(HEADS):
-        a, b, c = full[p]
-        for name in ("own", "sib", "ho"):
-            scr[name + str(p)] = vm(a, b, c)
         scr["xp" + str(p)] = vm(ny, zh_n) if p < 2 else vm(zh_n, ny)
+    for name in ("own", "sib", "ho"):
+        scr[name] = [vm(size[three], size[two], many) for _, _, many, two, three in pieces]
+    scr["start"] = [vm(n) for n in (ny, nz, ny)]
+    scr["ends"] = [vm(n) for n in (ny, nz, ny)]
+    scr["er"] = [vm(n - 1) for n in (ny, nz, ny)]
     scr["xmid"] = [vm(zh_n), vm(zh_n), vm(ny)]
     scr["xr"] = []
-    scr["gr"] = []
-    scr["gmid"] = []
     for p in range(HEADS):
         first, second = (ny, zh_n) if p < 2 else (zh_n, ny)
-        a, b, c = full[p]
         scr["xr"].append([vm(first - 1, second), vm(second - 1)])
-        scr["gr"].append([vm(a - 1, b, c), vm(b - 1, c), vm(c - 1)])
-        scr["gmid"].append([vm(b, c), vm(c)])
+    scr["gr"] = [
+        [vm(size[three] - 1, size[two], many), vm(size[two] - 1, many)]
+        for _, _, many, two, three in pieces
+    ]
+    scr["gmid"] = [vm(size[two], many) for _, _, many, two, three in pieces]
     return scr
 
 
@@ -482,19 +518,9 @@
     w_down,
 ):
     features = w_gate.shape[1]
-    smem = pl.BlockSpec(memory_space=pltpu.SMEM)
     vmem = pl.BlockSpec(memory_space=pltpu.VMEM)
     hbm = pl.BlockSpec(memory_space=pl.ANY)
-    return pl.pallas_call(
-        functools.partial(kernel, geom),
-        out_shape=jax.ShapeDtypeStruct(child_query.shape[:2] + (HEADS * LANES,), BF),
-        in_specs=[smem] * 3 + [vmem] * 4 + [hbm] * 4,
-        out_specs=vmem,
-        scratch_shapes=[scratch_of(geom, features)],
-        compiler_params=pltpu.CompilerParams(
-            collective_id=0, has_side_effects=True, vmem_limit_bytes=58 * 1024 * 1024
-        ),
-    )(
+    operands = [
         node_slot,
         routes.transpose(0, 2, 1),
         gate_w.transpose(0, 2, 1),
@@ -502,6 +528,20 @@
         child_query.transpose(0, 2, 1, 3),
         child_kv,
         node_hidden,
+    ]
+    held = [pltpu.SMEM(v.shape, v.dtype) for v in operands[:3]]
+    held += [pltpu.VMEM(v.shape, v.dtype) for v in operands[3:]]
+    return pl.pallas_call(
+        functools.partial(kernel, geom),
+        out_shape=jax.ShapeDtypeStruct(child_query.shape[:2] + (HEADS * LANES,), BF),
+        in_specs=[hbm] * (len(operands) + 4),
+        out_specs=vmem,
+        scratch_shapes=[scratch_of(geom, features, held)],
+        compiler_params=pltpu.CompilerParams(
+            collective_id=0, has_side_effects=True, vmem_limit_bytes=58 * 1024 * 1024
+        ),
+    )(
+        *operands,
         node_cache,
         w_gate,
         w_up,

time: 90.9 us -> 86.1 us (0.947)
  Pallas kernels: 89.4 us -> 84.6 us
    pallas_call x1, Pallas kernels: 89.4 us -> 84.6 us  [local(): pl.pallas_call(functools.partial(kernel, geom), out_shape=jax.ShapeDtypeS...]
where the time goes in v4:
time: 86.1 us; the launch traced here: 85.9 us
  Pallas kernels  84.6 us (98%)
  local copies, waits for them, and re-layouts  1.29 us (1%)
    pallas_call x1, Pallas kernels, local(): pl.pallas_call(functools.partial(kernel, geom), out_shape=jax.ShapeDtypeS...  84.6 us

profile of v4, /device:TPU:1, one launch (start us, length us, event | category | flops | bytes accessed | tf_op | source)
XLA Modules:
  0.0 85.9 jit_solution(3013351783751901619)
XLA Ops:
  0.0 84.6 %shard_map.109 = bf16[2,4,384]{2,1,0:T(4,128)(2,1)} custom-call(s32[32]{0:T(128)} %slot_ref.1, s32[2,2,4]{2,1,0:T(2,128)} %bitcast.5, f32[2,2,4]{2,1,0:T(2,128)} %bitcast.6, s32[1,64]{1,0:T(1,128)} %bitcast.7, bf16[2,3,4,128]{3,2,1,0:T(4,128)(2,1)} %bitcast.4, bf16[2,1,2,4,128]{4,3,2,1,0:T(4,128)(2,1)} %kv_ref.1, bf16[1,384]{1,0:T(2,128)(2,1)} %hid_ref.1, ...), custom_call_target="tpu_custom_call" | custom-call | tf_op jit(solution)/shard_map/pallas_call | solution.py:534
  84.6 1.3 %copy.13 = bf16[2,4,384]{2,1,0:T(4,128)(2,1)} copy(bf16[2,4,384]{2,1,0:T(4,128)(2,1)} %shard_map.109) | data formatting | bytes 12288

commit v5 on v4

--- a/solution.py
+++ b/solution.py
@@ -308,15 +308,17 @@
             start[p][firsts[p].me] = w
 
         yield from scatter(mids[p], xr[p][1], second, final)
-
-    interleave([home(p) for p in range(HEADS)])
+        yield from gather(start[p], firsts[p])
+
+    homes = [home(p) for p in range(HEADS)]
+    for _ in range(3):
+        for job in homes:
+            next(job)
 
     sib = scr["sib"]
     d2d = []
     rings = {"x": rx, "y": ry, "z": rz}
     pieces = pieces_of(geom)
-
-    interleave([gather(start[p], firsts[p]) for p in range(HEADS)])
 
     def everywhere(k):
         p, low, many, two, three = pieces[k]
@@ -334,7 +336,13 @@
         forward(three.me)
         yield from gather(own[k], three, forward)
 
-    interleave([everywhere(k) for k in range(len(pieces))])
+    spread = [everywhere(k) for k in range(len(pieces))]
+    for p in range(HEADS):
+        interleave([homes[p]])
+        for k in (0, 1, 2, 3, 4):
+            if pieces[k][0] == p:
+                next(spread[k])
+    interleave([spread[k] for k in (0, 2, 1, 3, 4)])
 
     def tiles(refs, p, xi, m, i):
         zi = i * zl_n + m
@@ -425,8 +433,6 @@
         yield from scatter(ho[k], gr[k][0], rings[three], keep)
         yield from scatter(gmid[k], gr[k][1], rings[two], end)
 
-    interleave([back(k) for k in range(len(pieces))])
-
     def last(p):
         def final(v):
             w = (xs[p].astype(F32) + v).astype(BF)
@@ -435,7 +441,17 @@
 
         yield from scatter(ends[p], er[p], firsts[p], final)
 
-    interleave([last(p) for p in range(HEADS)])
+    backs = [back(k) for k in range(len(pieces))]
+    lasts = [last(p) for p in range(HEADS)]
+    for k in (0, 2, 1, 3, 4):
+        next(backs[k])
+    for k in (1, 3, 4, 0, 2):
+        next(backs[k])
+    for k in (1, 3, 4, 0, 2):
+        interleave([backs[k]])
+        if k in (4, 0, 2):
+            next(lasts[pieces[k][0]])
+    interleave([lasts[p] for p in (2, 0, 1)])
 
     for ref, send in pending:
         transfer(ref, ref, sibling, send, 0).wait_send()

time: 86.1 us -> 84.4 us (0.980)
  Pallas kernels: 84.6 us -> 82.9 us
    pallas_call x1, Pallas kernels: 84.6 us -> 82.9 us  [local(): pl.pallas_call(functools.partial(kernel, geom), out_shape=jax.ShapeDtypeS...]
where the time goes in v5:
time: 84.4 us; the launch traced here: 84.2 us
  Pallas kernels  82.9 us (98%)
  local copies, waits for them, and re-layouts  1.29 us (2%)
    pallas_call x1, Pallas kernels, local(): pl.pallas_call(functools.partial(kernel, geom), out_shape=jax.ShapeDtypeS...  82.9 us

profile of v5, /device:TPU:1, one launch (start us, length us, event | category | flops | bytes accessed | tf_op | source)
XLA Modules:
  0.0 84.2 jit_solution(5339231789556743853)
XLA Ops:
  0.0 82.9 %shard_map.109 = bf16[2,4,384]{2,1,0:T(4,128)(2,1)} custom-call(s32[32]{0:T(128)} %slot_ref.1, s32[2,2,4]{2,1,0:T(2,128)} %bitcast.5, f32[2,2,4]{2,1,0:T(2,128)} %bitcast.6, s32[1,64]{1,0:T(1,128)} %bitcast.7, bf16[2,3,4,128]{3,2,1,0:T(4,128)(2,1)} %bitcast.4, bf16[2,1,2,4,128]{4,3,2,1,0:T(4,128)(2,1)} %kv_ref.1, bf16[1,384]{1,0:T(2,128)(2,1)} %hid_ref.1, ...), custom_call_target="tpu_custom_call" | custom-call | tf_op jit(solution)/shard_map/pallas_call | solution.py:550
  82.9 1.3 %copy.13 = bf16[2,4,384]{2,1,0:T(4,128)(2,1)} copy(bf16[2,4,384]{2,1,0:T(4,128)(2,1)} %shard_map.109) | data formatting | bytes 12288

commit v6 on v5

--- a/solution.py
+++ b/solution.py
@@ -135,6 +135,7 @@
                 index = ring.at(-k)
                 arrive(buf.at[index], recvs[k])
                 got(index)
+                yield
 
     def scatter(h, r, ring, finish):
         send, recv = next(next_send), next(next_recv)
@@ -149,6 +150,16 @@
             total = total + r[k].astype(F32)
         finish(total)
 
+    barrier = pltpu.get_barrier_semaphore()
+    far = [
+        (min(k, ring.size - k), ring.device(ring.at(k)))
+        for ring in (rz, ry, rx)
+        for k in range(1, ring.size)
+    ]
+    partners = [device for _, device in sorted(far, key=lambda entry: -entry[0])] + [sibling]
+    for partner in partners:
+        pl.semaphore_signal(barrier, inc=1, device_id=partner, device_id_type=pl.DeviceIdType.MESH)
+
     inputs = [slot_ref, routes_ref, gate_ref, parent_ref, query_ref, kv_ref, hid_ref]
     held = scr["held"]
     small = [
@@ -157,13 +168,6 @@
     ]
     for c in small:
         c.start()
-
-    barrier = pltpu.get_barrier_semaphore()
-    partners = [sibling]
-    for ring in (rx, ry, rz):
-        partners += [ring.device(ring.at(k)) for k in range(1, ring.size)]
-    for partner in partners:
-        pl.semaphore_signal(barrier, inc=1, device_id=partner, device_id_type=pl.DeviceIdType.MESH)
 
     loads = [
         pltpu.make_async_copy(wg_ref.at[0], scr["wgu"].at[:, pl.ds(0, LANES)], load_sems.at[0]),
@@ -264,6 +268,30 @@
     here_row = (token_child == child_id) & (parent_ref[...] == node)
     mine = jnp.sum(jnp.where(here_row, 1.0, 0.0), axis=1, keepdims=True)
     xp = [scr["xp0"], scr["xp1"], scr["xp2"]]
+    own = scr["own"]
+    start = scr["start"]
+    xr = scr["xr"]
+    mids = scr["xmid"]
+    xs = scr["xs"]
+    firsts = (ry, rz, ry)
+
+    def home(p):
+        first, second = (ry, rzh) if p < 2 else (rzh, ry)
+
+        def keep(v):
+            mids[p][...] = v.astype(BF)
+
+        yield from scatter(xp[p], xr[p][0], first, keep)
+
+        def final(v):
+            w = v.astype(BF)
+            xs[p] = w
+            start[p][firsts[p].me] = w
+
+        yield from scatter(mids[p], xr[p][1], second, final)
+        yield from gather(start[p], firsts[p])
+
+    homes = [home(p) for p in range(HEADS)]
     for p in range(HEADS):
         q = rows_a(p).astype(BF)
         s_old = lax.dot_general(q, old_k, contract, preferred_element_type=F32) * scale
@@ -286,32 +314,9 @@
                 xp[p][:, i] = here[i].astype(BF)
         else:
             xp[p][...] = here.astype(BF)
-
-    own = scr["own"]
-    start = scr["start"]
-    xr = scr["xr"]
-    mids = scr["xmid"]
-    xs = scr["xs"]
-    firsts = (ry, rz, ry)
-
-    def home(p):
-        first, second = (ry, rzh) if p < 2 else (rzh, ry)
-
-        def keep(v):
-            mids[p][...] = v.astype(BF)
-
-        yield from scatter(xp[p], xr[p][0], first, keep)
-
-        def final(v):
-            w = v.astype(BF)
-            xs[p] = w
-            start[p][firsts[p].me] = w
-
-        yield from scatter(mids[p], xr[p][1], second, final)
-        yield from gather(start[p], firsts[p])
-
-    homes = [home(p) for p in range(HEADS)]
-    for _ in range(3):
+        next(homes[p])
+
+    for _ in range(2):
         for job in homes:
             next(job)
 

time: 84.4 us -> 83 us (0.983)
  Pallas kernels: 82.9 us -> 81.6 us
    pallas_call x1, Pallas kernels: 82.9 us -> 81.6 us  [local(): pl.pallas_call(functools.partial(kernel, geom), out_shape=jax.ShapeDtypeS...]
where the time goes in v6:
time: 83 us; the launch traced here: 82.9 us
  Pallas kernels  81.6 us (98%)
  local copies, waits for them, and re-layouts  1.29 us (2%)
    pallas_call x1, Pallas kernels, local(): pl.pallas_call(functools.partial(kernel, geom), out_shape=jax.ShapeDtypeS...  81.6 us

profile of v6, /device:TPU:1, one launch (start us, length us, event | category | flops | bytes accessed | tf_op | source)
XLA Modules:
  0.0 82.9 jit_solution(14892114442393992958)
XLA Ops:
  0.0 81.6 %shard_map.109 = bf16[2,4,384]{2,1,0:T(4,128)(2,1)} custom-call(s32[32]{0:T(128)} %slot_ref.1, s32[2,2,4]{2,1,0:T(2,128)} %bitcast.5, f32[2,2,4]{2,1,0:T(2,128)} %bitcast.6, s32[1,64]{1,0:T(1,128)} %bitcast.7, bf16[2,3,4,128]{3,2,1,0:T(4,128)(2,1)} %bitcast.4, bf16[2,1,2,4,128]{4,3,2,1,0:T(4,128)(2,1)} %kv_ref.1, bf16[1,384]{1,0:T(2,128)(2,1)} %hid_ref.1, ...), custom_call_target="tpu_custom_call" | custom-call | tf_op jit(solution)/shard_map/pallas_call | solution.py:555
  81.6 1.3 %copy.13 = bf16[2,4,384]{2,1,0:T(4,128)(2,1)} copy(bf16[2,4,384]{2,1,0:T(4,128)(2,1)} %shard_map.109) | data formatting | bytes 12288

commit v7 on v6

--- a/solution.py
+++ b/solution.py
@@ -292,7 +292,8 @@
         yield from gather(start[p], firsts[p])
 
     homes = [home(p) for p in range(HEADS)]
-    for p in range(HEADS):
+    turns = (2, 0, 1)
+    for p in turns:
         q = rows_a(p).astype(BF)
         s_old = lax.dot_general(q, old_k, contract, preferred_element_type=F32) * scale
         s_new = lax.dot_general(q, new_k, contract, preferred_element_type=F32) * scale
@@ -317,8 +318,8 @@
         next(homes[p])
 
     for _ in range(2):
-        for job in homes:
-            next(job)
+        for p in turns:
+            next(homes[p])
 
     sib = scr["sib"]
     d2d = []
@@ -342,12 +343,12 @@
         yield from gather(own[k], three, forward)
 
     spread = [everywhere(k) for k in range(len(pieces))]
-    for p in range(HEADS):
+    for p in turns:
         interleave([homes[p]])
         for k in (0, 1, 2, 3, 4):
             if pieces[k][0] == p:
                 next(spread[k])
-    interleave([spread[k] for k in (0, 2, 1, 3, 4)])
+    interleave([spread[k] for k in (0, 2, 4, 1, 3)])
 
     def tiles(refs, p, xi, m, i):
         zi = i * zl_n + m
@@ -448,11 +449,11 @@
 
     backs = [back(k) for k in range(len(pieces))]
     lasts = [last(p) for p in range(HEADS)]
-    for k in (0, 2, 1, 3, 4):
+    for k in (4, 0, 2, 1, 3):
         next(backs[k])
-    for k in (1, 3, 4, 0, 2):
+    for k in (4, 1, 3, 0, 2):
         next(backs[k])
-    for k in (1, 3, 4, 0, 2):
+    for k in (4, 1, 3, 0, 2):
         interleave([backs[k]])
         if k in (4, 0, 2):
             next(lasts[pieces[k][0]])

time: 83 us -> 84.3 us (1.016)
  Pallas kernels: 81.6 us -> 82.8 us
    pallas_call x1, Pallas kernels: 81.6 us -> 82.8 us  [local(): pl.pallas_call(functools.partial(kernel, geom), out_shape=jax.ShapeDtypeS...]
where the time goes in v7:
time: 84.3 us; the launch traced here: 84.1 us
  Pallas kernels  82.8 us (98%)
  local copies, waits for them, and re-layouts  1.29 us (2%)
    pallas_call x1, Pallas kernels, local(): pl.pallas_call(functools.partial(kernel, geom), out_shape=jax.ShapeDtypeS...  82.8 us

profile of v7, /device:TPU:1, one launch (start us, length us, event | category | flops | bytes accessed | tf_op | source)
XLA Modules:
  0.0 84.1 jit_solution(10712804225237050344)
XLA Ops:
  0.0 82.8 %shard_map.109 = bf16[2,4,384]{2,1,0:T(4,128)(2,1)} custom-call(s32[32]{0:T(128)} %slot_ref.1, s32[2,2,4]{2,1,0:T(2,128)} %bitcast.5, f32[2,2,4]{2,1,0:T(2,128)} %bitcast.6, s32[1,64]{1,0:T(1,128)} %bitcast.7, bf16[2,3,4,128]{3,2,1,0:T(4,128)(2,1)} %bitcast.4, bf16[2,1,2,4,128]{4,3,2,1,0:T(4,128)(2,1)} %kv_ref.1, bf16[1,384]{1,0:T(2,128)(2,1)} %hid_ref.1, ...), custom_call_target="tpu_custom_call" | custom-call | tf_op jit(solution)/shard_map/pallas_call | solution.py:556
  82.8 1.3 %copy.13 = bf16[2,4,384]{2,1,0:T(4,128)(2,1)} copy(bf16[2,4,384]{2,1,0:T(4,128)(2,1)} %shard_map.109) | data formatting | bytes 12288
